TPU v7x, 32 devices: a whole 2x2x4 slice. The times are simulated.
32 devices in a mesh: seq: 8 (over z, x), batch: 4 (over y, core).
Axes of the slice: x: 2, y: 2, z: 4, core: 2. Of those that a mesh axis runs over, the one named last changes fastest.
Arguments:
- inputs: bfloat16 [2, 4, 2048, 768], P(None, 'batch', 'seq'), may hold values from -6 to 6
- cotangent: bfloat16 [2, 4, 2048, 768], P(None, 'batch', 'seq'), may hold values from -6 to 6
- doc_lengths: int32 [2, 4, 4], P(None, 'batch'), may hold values from 0 to 2048, as said below
- random_blocks: int32 [2, 4, 32, 3], P(None, 'batch'), may hold values from 0 to 31, as said below
- w_query: bfloat16 [768, 768], P(('seq', 'batch')), may hold values from -0.21875 to 0.21875
- w_key: bfloat16 [768, 768], P(('seq', 'batch')), may hold values from -0.21875 to 0.21875
- w_value: bfloat16 [768, 768], P(('seq', 'batch')), may hold values from -0.21875 to 0.21875
- w_out: bfloat16 [768, 768], P(('seq', 'batch')), may hold values from -0.875 to 0.875
- w_up: bfloat16 [768, 3072], P(('seq', 'batch')), may hold values from -0.21875 to 0.21875
- w_down: bfloat16 [3072, 768], P(('seq', 'batch')), may hold values from -0.109375 to 0.109375
- b_query: bfloat16 [768], P(('seq', 'batch')), may hold values from -3 to 3
- b_value: bfloat16 [768], P(('seq', 'batch')), may hold values from -3 to 3
- b_out: bfloat16 [768], P(('seq', 'batch')), may hold values from -3 to 3
- b_up: bfloat16 [3072], P(('seq', 'batch')), may hold values from -3 to 3
- b_down: bfloat16 [768], P(('seq', 'batch')), may hold values from -3 to 3
- gain_attn: bfloat16 [768], P(('seq', 'batch')), may hold values from 0.5 to 1.5
- bias_attn: bfloat16 [768], P(('seq', 'batch')), may hold values from -3 to 3
- gain_ffn: bfloat16 [768], P(('seq', 'batch')), may hold values from 0.5 to 1.5
- bias_ffn: bfloat16 [768], P(('seq', 'batch')), may hold values from -3 to 3
Outputs:
- outputs: bfloat16 [2, 4, 2048, 768], P(None, 'batch', 'seq')
- grad_inputs: float32 [2, 4, 2048, 768], P(None, 'batch', 'seq')
- grad_w_query: float32 [768, 768], P(('seq', 'batch'))
- grad_w_key: float32 [768, 768], P(('seq', 'batch'))
- grad_w_value: float32 [768, 768], P(('seq', 'batch'))
- grad_w_out: float32 [768, 768], P(('seq', 'batch'))
- grad_w_up: float32 [768, 3072], P(('seq', 'batch'))
- grad_w_down: float32 [3072, 768], P(('seq', 'batch'))
- grad_b_query: float32 [768], P(('seq', 'batch'))
- grad_b_value: float32 [768], P(('seq', 'batch'))
- grad_b_out: float32 [768], P(('seq', 'batch'))
- grad_b_up: float32 [3072], P(('seq', 'batch'))
- grad_b_down: float32 [768], P(('seq', 'batch'))
- grad_gain_attn: float32 [768], P(('seq', 'batch'))
- grad_bias_attn: float32 [768], P(('seq', 'batch'))
- grad_gain_ffn: float32 [768], P(('seq', 'batch'))
- grad_bias_ffn: float32 [768], P(('seq', 'batch'))
Inputs may be any that keep to these rules, and one draw needn't show every extreme that they name: `doc_lengths`: every entry is a multiple of 128 and the 4 entries of a sequence add up to 2048. For each sequence index s, in one micro-batch drawn from the seed sequence s is a single document: first entry 2048, the others 0; elsewhere all entries are positive. `random_blocks`: entry [m, s, d * 4 + j, r] names a block of sequence (m, s). With t = (m * 3 + r) * 4 + j, the device along seq that holds the named block (entry // 4) depends only on s, d and t modulo the number of devices along seq, and different residues give different devices. The 3 entries of one block differ.
All inputs are finite; a program needn't handle non-finite values.
Results may differ from a plain program's by a relative error of at most 0.014.
Values may be sent and summed in bfloat16 or wider, within the bound.
A program may use at most 320 MiB of HBM per device.

v0:
```python
import jax
import jax.numpy as jnp
from jax import lax
from jax.sharding import PartitionSpec as P

HD = 64
BLK = 64
WIN = 8
GLB = 2
RAND = 3


masked_value = -1e30
norm_epsilon = 1e-06


def shifted(x, axis, by):
    peers = lax.axis_size(axis)
    pairs = [(i, i + by) for i in range(peers) if 0 <= i + by < peers]
    return lax.ppermute(x, axis, pairs)


def doc_tables(lengths, positions):
    doc_ends = jnp.cumsum(lengths)
    starts = doc_ends - lengths
    counted = (doc_ends[None, :] <= positions[:, None]).astype(jnp.int32)
    doc_index = jnp.minimum(jnp.sum(counted, axis=1), lengths.shape[0] - 1)
    picked = jnp.arange(lengths.shape[0], dtype=jnp.int32)[None, :] == doc_index[:, None]
    doc_first = jnp.sum(jnp.where(picked, starts[None, :], 0), axis=1)
    return (doc_index, doc_first)


def mask_parts(lengths, query_pos, key_pos, query_block, rand_mine, seq_len):
    glob_rows = GLB * BLK
    key_clip = jnp.clip(key_pos, 0, seq_len - 1)
    doc_query, first_query = doc_tables(lengths, query_pos)
    doc_key, first_key = doc_tables(lengths, key_clip)
    nearby = (
        jnp.abs(jnp.floor_divide(key_pos, BLK)[None, :] - jnp.floor_divide(query_pos, BLK)[:, None])
        <= WIN
    )
    inside = (key_pos >= 0) & (key_pos < seq_len) & (key_clip - first_key >= glob_rows)
    window_mask = nearby & inside[None, :] & (doc_key[None, :] == doc_query[:, None])
    glob_doc = jnp.repeat(jnp.arange(lengths.shape[0], dtype=jnp.int32), glob_rows)
    glob_mask = glob_doc[None, :] == doc_query[:, None]
    doc_block = doc_tables(lengths, query_block * BLK)[0]
    rand_flat = rand_mine.reshape(-1) * BLK
    doc_rand, first_rand = doc_tables(lengths, rand_flat)
    rand_shape = rand_mine.shape
    rand_mask = (
        (doc_rand.reshape(rand_shape) == doc_block[:, None])
        & (jnp.abs(rand_mine - query_block[:, None]) > WIN)
        & ((rand_flat - first_rand).reshape(rand_shape) >= glob_rows)
    )
    rand_mask = jnp.repeat(rand_mask, BLK, axis=1)
    return (window_mask, glob_mask, rand_mask, doc_query, first_query)


def norm_forward(values_in, norm_gain, norm_shift):
    average = jnp.mean(values_in, axis=-1, keepdims=True)
    centred = values_in - average
    inverse = lax.rsqrt(jnp.mean(centred * centred, axis=-1, keepdims=True) + norm_epsilon)
    normed = centred * inverse
    return (normed * norm_gain + norm_shift, normed, inverse)


def norm_backward(incoming, normed, inverse, norm_gain):
    scaled = incoming * norm_gain
    return inverse * (
        scaled
        - jnp.mean(scaled, axis=-1, keepdims=True)
        - normed * jnp.mean(scaled * normed, axis=-1, keepdims=True)
    )


def outer_sum(left, right):
    return lax.dot_general(
        left, right, (((0,), (0,)), ((), ())), preferred_element_type=jnp.float32
    )


def back_dot(grad_rows, matrix):
    return lax.dot_general(
        grad_rows, matrix, (((1,), (1,)), ((), ())), preferred_element_type=jnp.float32
    )


def gelu_tanh(pre_act):
    return jax.nn.gelu(pre_act, approximate=True)


def pick_rows(source_rows, row_ids):
    return source_rows[row_ids]


def on_device(
    inputs,
    cotangent,
    doc_lengths,
    random_blocks,
    w_query,
    w_key,
    w_value,
    w_out,
    w_up,
    w_down,
    b_query,
    b_value,
    b_out,
    b_up,
    b_down,
    gain_attn,
    bias_attn,
    gain_ffn,
    bias_ffn,
):
    shards = (
        w_query,
        w_key,
        w_value,
        w_out,
        w_up,
        w_down,
        b_query,
        b_value,
        b_out,
        b_up,
        b_down,
        gain_attn,
        bias_attn,
        gain_ffn,
        bias_ffn,
    )
    gathered = (
        lax.all_gather(shards[0], ("seq", "batch"), axis=0, tiled=True),
        lax.all_gather(shards[1], ("seq", "batch"), axis=0, tiled=True),
        lax.all_gather(shards[2], ("seq", "batch"), axis=0, tiled=True),
        lax.all_gather(shards[3], ("seq", "batch"), axis=0, tiled=True),
        lax.all_gather(shards[4], ("seq", "batch"), axis=0, tiled=True),
        lax.all_gather(shards[5], ("seq", "batch"), axis=0, tiled=True),
        lax.all_gather(shards[6], ("seq", "batch"), axis=0, tiled=True),
        lax.all_gather(shards[7], ("seq", "batch"), axis=0, tiled=True),
        lax.all_gather(shards[8], ("seq", "batch"), axis=0, tiled=True),
        lax.all_gather(shards[9], ("seq", "batch"), axis=0, tiled=True),
        lax.all_gather(shards[10], ("seq", "batch"), axis=0, tiled=True),
        lax.all_gather(shards[11], ("seq", "batch"), axis=0, tiled=True),
        lax.all_gather(shards[12], ("seq", "batch"), axis=0, tiled=True),
        lax.all_gather(shards[13], ("seq", "batch"), axis=0, tiled=True),
        lax.all_gather(shards[14], ("seq", "batch"), axis=0, tiled=True),
    )
    (
        full_query,
        full_key,
        full_value,
        full_out,
        full_up,
        full_down,
        bias_query,
        bias_value,
        bias_out,
        bias_up,
        bias_down,
        gain_one,
        shift_one,
        gain_two,
        shift_two,
    ) = gathered
    micro_count = inputs.shape[0]
    seq_dev = inputs.shape[2]
    model_width = inputs.shape[3]
    head_count = model_width // HD
    dev_count = lax.axis_size("seq")
    device = lax.axis_index("seq")
    seq_len = seq_dev * dev_count
    blk_dev = seq_dev // BLK
    halo_rows = WIN * BLK
    glob_rows = GLB * BLK
    score_scale = HD ** (-0.5)
    slot_count = micro_count * RAND * blk_dev
    capacity = -(-slot_count // dev_count)
    residues = min(dev_count, slot_count)
    reach_count = -(-halo_rows // seq_dev)
    moves = list(range(reach_count, 0, -1)) + list(range(-1, -reach_count - 1, -1))
    tokens = inputs[:, 0]
    lengths_all = doc_lengths[:, 0]
    rand_all = random_blocks[:, 0]
    flat_x = tokens.reshape(micro_count * seq_dev, model_width)
    kv_width = 2 * model_width
    queries = (
        jnp.dot(flat_x, full_query, preferred_element_type=jnp.float32)
        + bias_query.astype(jnp.float32)
    ).astype(jnp.bfloat16)
    key_rows = jnp.dot(flat_x, full_key, preferred_element_type=jnp.float32).astype(jnp.bfloat16)
    values = (
        jnp.dot(flat_x, full_value, preferred_element_type=jnp.float32)
        + bias_value.astype(jnp.float32)
    ).astype(jnp.bfloat16)
    key_value = jnp.concatenate([key_rows, values], axis=1).reshape(micro_count, seq_dev, kv_width)
    arrived = {}
    for offset in moves:
        arrived[offset] = shifted(key_value, "seq", offset)
    left_rim = jnp.concatenate([arrived[step] for step in range(reach_count, 0, -1)], axis=1)
    right_rim = jnp.concatenate([arrived[-step] for step in range(1, reach_count + 1)], axis=1)
    window_all = jnp.concatenate([left_rim, key_value, right_rim], axis=1)
    ends_all = jnp.cumsum(lengths_all, axis=1)
    starts_all = ends_all - lengths_all
    glob_local = (
        starts_all[:, :, None] + jnp.arange(glob_rows, dtype=jnp.int32)[None, None, :]
    ).reshape(micro_count, -1) - device * seq_dev
    owned = (
        (glob_local >= 0) & (glob_local < seq_dev) & jnp.repeat(lengths_all > 0, glob_rows, axis=1)
    )
    picked_rows = jax.vmap(pick_rows)(key_value, jnp.clip(glob_local, 0, seq_dev - 1))
    glob_table = jnp.where(owned[..., None], picked_rows.astype(jnp.float32), 0.0).reshape(
        -1, kv_width
    )
    glob_part = lax.psum_scatter(glob_table, "seq", scatter_dimension=0, tiled=True).astype(
        jnp.bfloat16
    )
    glob_kv = lax.all_gather(glob_part, "seq", axis=0, tiled=True).reshape(
        micro_count, -1, kv_width
    )
    rand_dev = (
        rand_all.reshape(micro_count, dev_count, blk_dev, RAND)
        .transpose(1, 0, 3, 2)
        .reshape(dev_count, slot_count)
    )
    source_dev = jnp.floor_divide(rand_dev, blk_dev)
    padded_ids = jnp.pad(rand_dev, ((0, 0), (0, capacity * dev_count - slot_count))).reshape(
        dev_count, capacity, dev_count
    )
    slot_grid = jnp.arange(capacity * dev_count, dtype=jnp.int32).reshape(capacity, dev_count)
    live_slot = slot_grid < slot_count
    matched = jnp.pad(source_dev[:, :residues] == device, ((0, 0), (0, dev_count - residues)))
    chosen = matched[:, None, :] & live_slot[None, :, :]
    block_ids = (
        jnp.floor_divide(slot_grid, RAND * blk_dev)[None] * blk_dev + padded_ids - device * blk_dev
    )
    send_index = jnp.sum(jnp.where(chosen, block_ids, 0), axis=2)
    send_live = jnp.any(chosen, axis=2)
    block_rows = key_value.reshape(micro_count * blk_dev, BLK, kv_width)
    outgoing = jnp.where(
        send_live[:, :, None, None], block_rows[send_index], jnp.zeros((), jnp.bfloat16)
    )
    incoming = lax.all_to_all(outgoing, "seq", split_axis=0, concat_axis=0, tiled=True)
    my_source = lax.dynamic_index_in_dim(source_dev, device, 0, keepdims=False)
    recv_index = my_source * capacity + jnp.floor_divide(
        jnp.arange(slot_count, dtype=jnp.int32), dev_count
    )
    rand_kv = incoming.reshape(dev_count * capacity, BLK, kv_width)[recv_index]
    rand_kv = (
        rand_kv.reshape(micro_count, RAND, blk_dev, BLK, kv_width)
        .transpose(0, 2, 1, 3, 4)
        .reshape(micro_count, blk_dev, RAND * BLK, kv_width)
    )

    def scores_of(query_heads, head_set, mask_set):
        window_keys, window_vals, glob_keys, glob_vals, rand_keys, rand_vals = head_set
        window_mask, glob_mask, rand_mask = (mask_set[0], mask_set[1], mask_set[2])
        window_scores = (
            jnp.einsum("qhd,khd->hqk", query_heads, window_keys, preferred_element_type=jnp.float32)
            * score_scale
        )
        window_scores = jnp.where(window_mask[None], window_scores, masked_value)
        glob_scores = (
            jnp.einsum("qhd,khd->hqk", query_heads, glob_keys, preferred_element_type=jnp.float32)
            * score_scale
        )
        glob_scores = jnp.where(glob_mask[None], glob_scores, masked_value)
        block_heads = query_heads.reshape(blk_dev, BLK, head_count, HD)
        rand_scores = (
            jnp.einsum(
                "jqhd,jkhd->hjqk", block_heads, rand_keys, preferred_element_type=jnp.float32
            )
            * score_scale
        )
        rand_scores = jnp.where(rand_mask[None, :, None, :], rand_scores, masked_value)
        return (window_scores, glob_scores, rand_scores)

    def probabilities(score_set, log_norm):
        window_scores, glob_scores, rand_scores = score_set
        return (
            jnp.exp(window_scores - log_norm[..., None]),
            jnp.exp(glob_scores - log_norm[..., None]),
            jnp.exp(rand_scores - log_norm.reshape(head_count, blk_dev, BLK)[..., None]),
        )

    query_pos = device * seq_dev + jnp.arange(seq_dev, dtype=jnp.int32)
    key_pos = device * seq_dev - halo_rows + jnp.arange(seq_dev + 2 * halo_rows, dtype=jnp.int32)
    query_block = device * blk_dev + jnp.arange(blk_dev, dtype=jnp.int32)
    kept_attn = []
    attended_list = []
    for micro_index in range(micro_count):
        rand_mine = lax.dynamic_slice_in_dim(rand_all[micro_index], device * blk_dev, blk_dev, 0)
        mask_set = mask_parts(
            lengths_all[micro_index], query_pos, key_pos, query_block, rand_mine, seq_len
        )
        query_heads = queries[micro_index * seq_dev : (micro_index + 1) * seq_dev].reshape(
            seq_dev, head_count, HD
        )
        window_kv = window_all[micro_index]
        glob_piece = glob_kv[micro_index]
        rand_piece = rand_kv[micro_index]
        split_window_keys = window_kv[:, :model_width].reshape(-1, head_count, HD)
        split_window_vals = window_kv[:, model_width:].reshape(-1, head_count, HD)
        split_glob_keys = glob_piece[:, :model_width].reshape(-1, head_count, HD)
        split_glob_vals = glob_piece[:, model_width:].reshape(-1, head_count, HD)
        split_rand_keys = rand_piece[:, :, :model_width].reshape(
            blk_dev, RAND * BLK, head_count, HD
        )
        split_rand_vals = rand_piece[:, :, model_width:].reshape(
            blk_dev, RAND * BLK, head_count, HD
        )
        head_set = (
            split_window_keys,
            split_window_vals,
            split_glob_keys,
            split_glob_vals,
            split_rand_keys,
            split_rand_vals,
        )
        score_set = scores_of(query_heads, head_set, mask_set)
        log_window_scores, log_glob_scores, log_rand_scores = score_set
        rand_flat = log_rand_scores.reshape(head_count, seq_dev, -1)
        top_score = jnp.maximum(
            jnp.maximum(jnp.max(log_window_scores, axis=-1), jnp.max(log_glob_scores, axis=-1)),
            jnp.max(rand_flat, axis=-1),
        )
        row_total = jnp.sum(jnp.exp(log_window_scores - top_score[..., None]), axis=-1)
        row_total = row_total + jnp.sum(jnp.exp(log_glob_scores - top_score[..., None]), axis=-1)
        row_total = row_total + jnp.sum(jnp.exp(rand_flat - top_score[..., None]), axis=-1)
        log_norm = top_score + jnp.log(row_total)
        prob_window, prob_glob, prob_rand = probabilities(score_set, log_norm)
        summed = jnp.einsum(
            "hqk,khd->qhd",
            prob_window.astype(jnp.bfloat16),
            head_set[1],
            preferred_element_type=jnp.float32,
        )
        summed = summed + jnp.einsum(
            "hqk,khd->qhd",
            prob_glob.astype(jnp.bfloat16),
            head_set[3],
            preferred_element_type=jnp.float32,
        )
        summed = summed + jnp.einsum(
            "hjqk,jkhd->jqhd",
            prob_rand.astype(jnp.bfloat16),
            head_set[5],
            preferred_element_type=jnp.float32,
        ).reshape(seq_dev, head_count, HD)
        attended_list.append(summed.reshape(seq_dev, model_width).astype(jnp.bfloat16))
        kept_attn.append((mask_set, log_norm, query_heads, head_set))
    attended = jnp.concatenate(attended_list, axis=0)
    gain_one_f = gain_one.astype(jnp.float32)
    gain_two_f = gain_two.astype(jnp.float32)
    branch = jnp.dot(attended, full_out, preferred_element_type=jnp.float32) + bias_out.astype(
        jnp.float32
    )
    middle, normed_one, inverse_one = norm_forward(
        flat_x.astype(jnp.float32) + branch, gain_one_f, shift_one.astype(jnp.float32)
    )
    middle_low = middle.astype(jnp.bfloat16)
    pre_act = jnp.dot(middle_low, full_up, preferred_element_type=jnp.float32) + bias_up.astype(
        jnp.float32
    )
    kept_hidden = gelu_tanh(pre_act).astype(jnp.bfloat16)
    ffn_out = jnp.dot(
        kept_hidden, full_down, preferred_element_type=jnp.float32
    ) + bias_down.astype(jnp.float32)
    result_rows, normed_two, inverse_two = norm_forward(
        middle + ffn_out, gain_two_f, shift_two.astype(jnp.float32)
    )
    outputs = result_rows.astype(jnp.bfloat16).reshape(micro_count, 1, seq_dev, model_width)
    regathered = (
        lax.all_gather(shards[0], ("seq", "batch"), axis=0, tiled=True),
        lax.all_gather(shards[1], ("seq", "batch"), axis=0, tiled=True),
        lax.all_gather(shards[2], ("seq", "batch"), axis=0, tiled=True),
        lax.all_gather(shards[3], ("seq", "batch"), axis=0, tiled=True),
        lax.all_gather(shards[4], ("seq", "batch"), axis=0, tiled=True),
        lax.all_gather(shards[5], ("seq", "batch"), axis=0, tiled=True),
        lax.all_gather(shards[6], ("seq", "batch"), axis=0, tiled=True),
        lax.all_gather(shards[7], ("seq", "batch"), axis=0, tiled=True),
        lax.all_gather(shards[8], ("seq", "batch"), axis=0, tiled=True),
        lax.all_gather(shards[9], ("seq", "batch"), axis=0, tiled=True),
        lax.all_gather(shards[10], ("seq", "batch"), axis=0, tiled=True),
        lax.all_gather(shards[11], ("seq", "batch"), axis=0, tiled=True),
        lax.all_gather(shards[12], ("seq", "batch"), axis=0, tiled=True),
        lax.all_gather(shards[13], ("seq", "batch"), axis=0, tiled=True),
        lax.all_gather(shards[14], ("seq", "batch"), axis=0, tiled=True),
    )
    (
        back_query,
        back_key,
        back_value,
        back_out,
        back_up,
        back_down,
        back_bias_query,
        back_bias_value,
        back_bias_out,
        back_bias_up,
        back_bias_down,
        back_gain_one,
        back_shift_one,
        back_gain_two,
        back_shift_two,
    ) = regathered
    cot_flat = cotangent[:, 0].reshape(-1, model_width).astype(jnp.float32)
    grad_gain_two = jnp.sum(cot_flat * normed_two, axis=0)
    grad_shift_two = jnp.sum(cot_flat, axis=0)
    d_second = norm_backward(cot_flat, normed_two, inverse_two, back_gain_two.astype(jnp.float32))
    d_ffn = d_second.astype(jnp.bfloat16)
    grad_bias_down = jnp.sum(d_ffn, axis=0, dtype=jnp.float32)
    hidden_pre, hidden = (pre_act, kept_hidden)
    grad_down = outer_sum(hidden, d_ffn)
    d_hidden = back_dot(d_ffn, back_down)
    gelu_pull = jax.vjp(gelu_tanh, hidden_pre)[1]
    d_pre = gelu_pull(d_hidden)[0].astype(jnp.bfloat16)
    grad_bias_up = jnp.sum(d_pre, axis=0, dtype=jnp.float32)
    grad_up = outer_sum(middle_low, d_pre)
    d_middle = d_second + back_dot(d_pre, back_up)
    grad_gain_one = jnp.sum(d_middle * normed_one, axis=0)
    grad_shift_one = jnp.sum(d_middle, axis=0)
    d_first = norm_backward(d_middle, normed_one, inverse_one, back_gain_one.astype(jnp.float32))
    d_branch = d_first.astype(jnp.bfloat16)
    grad_bias_out = jnp.sum(d_branch, axis=0, dtype=jnp.float32)
    grad_out = outer_sum(attended, d_branch)
    d_attended = back_dot(d_branch, back_out).astype(jnp.bfloat16)
    grad_query_list = []
    window_grads = []
    glob_grads = []
    rand_grads = []
    for micro_index in range(micro_count):
        mask_set, log_norm, query_heads, head_set = kept_attn[micro_index]
        window_keys, window_vals, glob_keys, glob_vals, rand_keys, rand_vals = head_set
        score_set = scores_of(query_heads, head_set, mask_set)
        prob_window, prob_glob, prob_rand = probabilities(score_set, log_norm)
        grad_heads = d_attended[micro_index * seq_dev : (micro_index + 1) * seq_dev].reshape(
            seq_dev, head_count, HD
        )
        grad_blocks = grad_heads.reshape(blk_dev, BLK, head_count, HD)
        block_heads = query_heads.reshape(blk_dev, BLK, head_count, HD)
        dp_window = jnp.einsum(
            "qhd,khd->hqk", grad_heads, window_vals, preferred_element_type=jnp.float32
        )
        dp_glob = jnp.einsum(
            "qhd,khd->hqk", grad_heads, glob_vals, preferred_element_type=jnp.float32
        )
        dp_rand = jnp.einsum(
            "jqhd,jkhd->hjqk", grad_blocks, rand_vals, preferred_element_type=jnp.float32
        )
        row_delta = (
            jnp.sum(prob_window * dp_window, axis=-1)
            + jnp.sum(prob_glob * dp_glob, axis=-1)
            + jnp.sum(prob_rand * dp_rand, axis=-1).reshape(head_count, seq_dev)
        )
        ds_window = (prob_window * (dp_window - row_delta[..., None])).astype(jnp.bfloat16)
        ds_glob = (prob_glob * (dp_glob - row_delta[..., None])).astype(jnp.bfloat16)
        ds_rand = (
            prob_rand * (dp_rand - row_delta.reshape(head_count, blk_dev, BLK)[..., None])
        ).astype(jnp.bfloat16)
        grad_query = jnp.einsum(
            "hqk,khd->qhd", ds_window, window_keys, preferred_element_type=jnp.float32
        )
        grad_query = grad_query + jnp.einsum(
            "hqk,khd->qhd", ds_glob, glob_keys, preferred_element_type=jnp.float32
        )
        grad_query = grad_query + jnp.einsum(
            "hjqk,jkhd->jqhd", ds_rand, rand_keys, preferred_element_type=jnp.float32
        ).reshape(seq_dev, head_count, HD)
        grad_query_list.append((grad_query * score_scale).reshape(seq_dev, model_width))
        window_key_grad = (
            jnp.einsum("hqk,qhd->khd", ds_window, query_heads, preferred_element_type=jnp.float32)
            * score_scale
        )
        window_val_grad = jnp.einsum(
            "hqk,qhd->khd",
            prob_window.astype(jnp.bfloat16),
            grad_heads,
            preferred_element_type=jnp.float32,
        )
        window_grads.append(
            jnp.concatenate(
                [
                    window_key_grad.reshape(-1, model_width),
                    window_val_grad.reshape(-1, model_width),
                ],
                axis=1,
            )
        )
        glob_key_grad = (
            jnp.einsum("hqk,qhd->khd", ds_glob, query_heads, preferred_element_type=jnp.float32)
            * score_scale
        )
        glob_val_grad = jnp.einsum(
            "hqk,qhd->khd",
            prob_glob.astype(jnp.bfloat16),
            grad_heads,
            preferred_element_type=jnp.float32,
        )
        glob_grads.append(
            jnp.concatenate(
                [glob_key_grad.reshape(-1, model_width), glob_val_grad.reshape(-1, model_width)],
                axis=1,
            )
        )
        rand_key_grad = (
            jnp.einsum("hjqk,jqhd->jkhd", ds_rand, block_heads, preferred_element_type=jnp.float32)
            * score_scale
        )
        rand_val_grad = jnp.einsum(
            "hjqk,jqhd->jkhd",
            prob_rand.astype(jnp.bfloat16),
            grad_blocks,
            preferred_element_type=jnp.float32,
        )
        rand_grads.append(
            jnp.concatenate(
                [
                    rand_key_grad.reshape(blk_dev, RAND * BLK, model_width),
                    rand_val_grad.reshape(blk_dev, RAND * BLK, model_width),
                ],
                axis=2,
            )
        )
    window_grad = jnp.stack(window_grads)
    glob_grad = jnp.stack(glob_grads)
    rand_grad = jnp.stack(rand_grads)
    left_grad = window_grad[:, :halo_rows].reshape(micro_count, reach_count, seq_dev, kv_width)
    right_grad = window_grad[:, halo_rows + seq_dev :].reshape(
        micro_count, reach_count, seq_dev, kv_width
    )
    kv_grad = window_grad[:, halo_rows : halo_rows + seq_dev]
    for offset in moves:
        rim_piece = left_grad[:, reach_count + offset] if offset < 0 else right_grad[:, offset - 1]
        kv_grad = kv_grad + shifted(rim_piece.astype(jnp.bfloat16), "seq", offset).astype(
            rim_piece.dtype
        )
    glob_share_grad = lax.psum_scatter(
        glob_grad.reshape(-1, kv_width), "seq", scatter_dimension=0, tiled=True
    )
    glob_total = (
        lax.all_gather(glob_share_grad.astype(jnp.bfloat16), "seq", axis=0, tiled=True)
        .astype(glob_share_grad.dtype)
        .reshape(micro_count, -1, kv_width)
    )
    for micro_index in range(micro_count):
        doc_query, first_query = (kept_attn[micro_index][0][3], kept_attn[micro_index][0][4])
        inner = query_pos - first_query
        glob_index = doc_query * glob_rows + jnp.clip(inner, 0, glob_rows - 1)
        glob_rows_back = glob_total[micro_index][glob_index]
        kv_grad = kv_grad.at[micro_index].add(
            jnp.where((inner < glob_rows)[:, None], glob_rows_back, 0.0)
        )
    back_rows = (
        rand_grad.reshape(micro_count, blk_dev, RAND, BLK, kv_width)
        .transpose(0, 2, 1, 3, 4)
        .reshape(slot_count, BLK, kv_width)
    )
    back_buffer = (
        jnp.zeros((dev_count * capacity, BLK, kv_width), jnp.float32)
        .at[recv_index]
        .set(back_rows)
        .reshape(dev_count, capacity, BLK, kv_width)
    )
    returned = lax.all_to_all(
        back_buffer.astype(jnp.bfloat16), "seq", split_axis=0, concat_axis=0, tiled=True
    ).astype(back_buffer.dtype)
    returned = jnp.where(send_live[:, :, None, None], returned, 0.0).reshape(-1, BLK, kv_width)
    block_grad = (
        jnp.zeros((micro_count * blk_dev, BLK, kv_width), jnp.float32)
        .at[send_index.reshape(-1)]
        .add(returned)
    )
    kv_grad = kv_grad + block_grad.reshape(micro_count, seq_dev, kv_width)
    kv_flat = kv_grad.reshape(micro_count * seq_dev, kv_width)
    dq_low = jnp.concatenate(grad_query_list, axis=0).astype(jnp.bfloat16)
    dk_low = kv_flat[:, :model_width].astype(jnp.bfloat16)
    dv_low = kv_flat[:, model_width:].astype(jnp.bfloat16)
    grad_query_w = outer_sum(flat_x, dq_low)
    grad_key_w = outer_sum(flat_x, dk_low)
    grad_value_w = outer_sum(flat_x, dv_low)
    grad_bias_query = jnp.sum(dq_low, axis=0, dtype=jnp.float32)
    grad_bias_value = jnp.sum(dv_low, axis=0, dtype=jnp.float32)
    d_inputs = (
        d_first
        + back_dot(dq_low, back_query)
        + back_dot(dk_low, back_key)
        + back_dot(dv_low, back_value)
    )
    grad_inputs = d_inputs.reshape(micro_count, 1, seq_dev, model_width)
    summed_grads = (
        lax.psum_scatter(grad_query_w, ("seq", "batch"), scatter_dimension=0, tiled=True),
        lax.psum_scatter(grad_key_w, ("seq", "batch"), scatter_dimension=0, tiled=True),
        lax.psum_scatter(grad_value_w, ("seq", "batch"), scatter_dimension=0, tiled=True),
        lax.psum_scatter(grad_out, ("seq", "batch"), scatter_dimension=0, tiled=True),
        lax.psum_scatter(grad_up, ("seq", "batch"), scatter_dimension=0, tiled=True),
        lax.psum_scatter(grad_down, ("seq", "batch"), scatter_dimension=0, tiled=True),
        lax.psum_scatter(grad_bias_query, ("seq", "batch"), scatter_dimension=0, tiled=True),
        lax.psum_scatter(grad_bias_value, ("seq", "batch"), scatter_dimension=0, tiled=True),
        lax.psum_scatter(grad_bias_out, ("seq", "batch"), scatter_dimension=0, tiled=True),
        lax.psum_scatter(grad_bias_up, ("seq", "batch"), scatter_dimension=0, tiled=True),
        lax.psum_scatter(grad_bias_down, ("seq", "batch"), scatter_dimension=0, tiled=True),
        lax.psum_scatter(grad_gain_one, ("seq", "batch"), scatter_dimension=0, tiled=True),
        lax.psum_scatter(grad_shift_one, ("seq", "batch"), scatter_dimension=0, tiled=True),
        lax.psum_scatter(grad_gain_two, ("seq", "batch"), scatter_dimension=0, tiled=True),
        lax.psum_scatter(grad_shift_two, ("seq", "batch"), scatter_dimension=0, tiled=True),
    )
    return (outputs, grad_inputs) + tuple(summed_grads)


def solution(mesh):
    in_specs = (
        P(None, "batch", "seq", None),
        P(None, "batch", "seq", None),
        P(None, "batch", None),
        P(None, "batch", None, None),
        P(("seq", "batch"), None),
        P(("seq", "batch"), None),
        P(("seq", "batch"), None),
        P(("seq", "batch"), None),
        P(("seq", "batch"), None),
        P(("seq", "batch"), None),
        P(("seq", "batch")),
        P(("seq", "batch")),
        P(("seq", "batch")),
        P(("seq", "batch")),
        P(("seq", "batch")),
        P(("seq", "batch")),
        P(("seq", "batch")),
        P(("seq", "batch")),
        P(("seq", "batch")),
    )
    out_specs = (
        P(None, "batch", "seq", None),
        P(None, "batch", "seq", None),
        P(("seq", "batch"), None),
        P(("seq", "batch"), None),
        P(("seq", "batch"), None),
        P(("seq", "batch"), None),
        P(("seq", "batch"), None),
        P(("seq", "batch"), None),
        P(("seq", "batch")),
        P(("seq", "batch")),
        P(("seq", "batch")),
        P(("seq", "batch")),
        P(("seq", "batch")),
        P(("seq", "batch")),
        P(("seq", "batch")),
        P(("seq", "batch")),
        P(("seq", "batch")),
    )
    return jax.shard_map(
        on_device, mesh=mesh, in_specs=in_specs, out_specs=out_specs, check_vma=False
    )
```

profile of v0, /device:TPU:0, one launch (start us, length us, event | category | flops | bytes accessed | tf_op | source)
XLA Modules:
  0.0 1759.7 jit_solution(16423581789518998703)
XLA Ops:
  16.3 42.4 %all-reduce.19 = (bf16[768]{0:T(1024)(128)(2,1)S(1)}, bf16[768]{0:T(1024)(128)(2,1)S(1)}, bf16[768]{0:T(1024)(128)(2,1)S(1)}, bf16[768]{0:T(1024)(128)(2,1)S(1)}...) all-reduce(bf16[768]{0:T(1024)(128)(2,1)S(1)} %dynamic-update-slice, ...), channel_id=1, replica_groups=mesh['seq'=8,'batch'=4] {'seq','batch'}, use_global_device_ids=true, to_apply=%add.2 | all-reduce | flops 9216 | bytes 36864
  70.1 53.6 %all-gather.11.cloned.1.call-done = bf16[768,768]{1,0:T(8,128)(2,1)} async-done(((bf16[24,768]{1,0:T(8,128)(2,1)}), bf16[768,768]{1,0:T(8,128)(2,1)}) %all-gather.11.cloned.1.call-update) | async-done | bytes 1179664 | tf_op jit(solution)/shard_map/all_gather | solution.py:137
  126.0 19.0 %gather_fusion.4 = bf16[1024,1536]{1,0:T(8,128)(2,1)} fusion(bf16[2,256,1536]{2,1,0:T(8,128)(2,1)S(1)} %bitcast.368, s32[1024]{0:T(1024)S(1)} %bitcast.386), kind=kCustom, calls=%fused_computation.4 | custom fusion | bytes 6299648 | tf_op jit(solution)/shard_map/vmap()/gather | solution.py:93
  150.6 116.5 %reduce-scatter.15.cloned.1.call-done = f32[128,1536]{1,0:T(8,128)} async-done(((f32[1024,1536]{1,0:T(8,128)}), f32[128,1536]{1,0:T(8,128)}) %reduce-scatter.15.cloned.1.call-update) | async-done | bytes 786448 | tf_op jit(solution)/shard_map/reduce_scatter | solution.py:217
  308.9 89.1 %all-gather.13.cloned.1.call-done = bf16[768,768]{1,0:T(8,128)(2,1)} async-done(((bf16[24,768]{1,0:T(8,128)(2,1)}), bf16[768,768]{1,0:T(8,128)(2,1)}) %all-gather.13.cloned.1.call-update) | async-done | bytes 1179664 | tf_op jit(solution)/shard_map/all_gather | solution.py:135
  413.5 52.5 %collective-permute-done.3 = bf16[2,256,1536]{2,1,0:T(8,128)(2,1)} collective-permute-done((bf16[2,256,1536]{2,1,0:T(8,128)(2,1)S(1)}, bf16[2,256,1536]{2,1,0:T(8,128)(2,1)}, u32[]{:S(2)}, u32[]{:S(2)}) %collective-permute-start.3) | collective-permute-done | bytes 1572896 | tf_op jit(solution)/shard_map/ppermute | solution.py:20
  546.7 18.5 %exponential_reduce_fusion.1 = f32[12,256]{1,0:T(8,128)} fusion(f32[12,256,1280]{2,1,0:T(8,128)} %get-tuple-element.232, f32[12,256]{1,0:T(8,128)S(1)} %get-tuple-element.168, pred[256,1280]{1,0:T(8,128)(4,1)S(1)} %copy-done.34), kind=kLoop, calls=%fused_computation.15 | loop fusion | flops 15725568 | bytes 16080896 | tf_op jit(solution)/shard_map/reduce_sum | solution.py:329
  652.2 18.7 %all-gather.21.cloned.1.call-done = bf16[3072,768]{1,0:T(8,128)(2,1)} async-done(((bf16[96,768]{1,0:T(8,128)(2,1)}), bf16[3072,768]{1,0:T(8,128)(2,1)}) %all-gather.21.cloned.1.call-update) | async-done | bytes 4718608 | tf_op jit(solution)/shard_map/all_gather | solution.py:140
  705.9 12.9 multiply_reduce_fusion.1
  727.7 12.9 multiply_reduce_fusion
  786.0 137.8 %reduce-scatter.17.cloned.1.call-done = f32[128,1536]{1,0:T(8,128)} async-done(((f32[1024,1536]{1,0:T(8,128)}), f32[128,1536]{1,0:T(8,128)}) %reduce-scatter.17.cloned.1.call-update) | async-done | bytes 786448 | tf_op jit(solution)/shard_map/reduce_scatter | solution.py:540
  952.8 12.1 multiply_convert_fusion.1
  972.0 11.8 multiply_convert_fusion
  1087.9 19.6 %scatter_fusion = f32[24,64,1536]{2,1,0:T(8,128)} fusion(f32[24,64,1536]{2,1,0:T(8,128)} %broadcast_in_dim.358, s32[24]{0:T(128)S(1)} %copy-done.145, f32[24,64,1536]{2,1,0:T(8,128)} %bitcast.388), kind=kCustom, calls=%fused_computation.5 | custom fusion | bytes 28311648 | tf_op jit(solution)/shard_map/scatter | solution.py:564
  1118.9 10.3 fusion.131
  1142.7 9.8 fusion.83
  1214.2 27.8 %collective-permute-done.4 = bf16[2,256,1536]{2,1,0:T(8,128)(2,1)S(1)} collective-permute-done((bf16[2,256,1536]{2,1,0:T(8,128)(2,1)}, bf16[2,256,1536]{2,1,0:T(8,128)(2,1)S(1)}, u32[]{:S(2)}, u32[]{:S(2)}) %collective-permute-start.4) | collective-permute-done | bytes 1572896 | tf_op jit(solution)/shard_map/ppermute | solution.py:20
  1241.9 42.7 %collective-permute-done.5 = bf16[2,256,1536]{2,1,0:T(8,128)(2,1)S(1)} collective-permute-done((bf16[2,256,1536]{2,1,0:T(8,128)(2,1)}, bf16[2,256,1536]{2,1,0:T(8,128)(2,1)S(1)}, u32[]{:S(2)}, u32[]{:S(2)}) %collective-permute-start.5) | collective-permute-done | bytes 1572896 | tf_op jit(solution)/shard_map/ppermute | solution.py:20
  1284.7 16.9 collective-permute-done.7
  1315.2 13.8 scatter_fusion.1
  1366.1 40.0 %all-reduce.18 = (f32[768]{0:T(1024)S(1)}, f32[768]{0:T(1024)S(1)}, f32[768]{0:T(1024)S(1)}, f32[3072]{0:T(1024)S(1)}, f32[768]{0:T(1024)S(1)}, /*index=5*/f32[7...) all-reduce(f32[768]{0:T(1024)S(1)} %convert_reduce_fusion.5, ...), channel_id=10, replica_groups=mesh['seq'=8,'batch'=4] {'seq','batch'}, use_global_device_ids=true, to_apply=%region_57.58.clone | all-reduce | flops 9216 | bytes 73728
  1415.6 128.8 %reduce-scatter.23.cloned.1.call-done = f32[96,768]{1,0:T(8,128)} async-done(((f32[3072,768]{1,0:T(8,128)}), f32[96,768]{1,0:T(8,128)}) %reduce-scatter.23.cloned.1.call-update) | async-done | bytes 294928 | tf_op jit(solution)/shard_map/reduce_scatter | solution.py:599
  1544.4 103.7 %reduce-scatter.27.cloned.1.call-done = f32[24,768]{1,0:T(8,128)} async-done(((f32[768,768]{1,0:T(8,128)}), f32[24,768]{1,0:T(8,128)}) %reduce-scatter.27.cloned.1.call-update) | async-done | bytes 73744
  1648.1 104.6 %reduce-scatter.29.cloned.1.call-done = f32[24,768]{1,0:T(8,128)} async-done(((f32[768,768]{1,0:T(8,128)}), f32[24,768]{1,0:T(8,128)}) %reduce-scatter.29.cloned.1.call-update) | async-done | bytes 73744
  (715 shorter events, 627.2 us)
Async XLA Ops:
  7.9 115.8 %all-gather.11.cloned.1.call-start = ((), (), s32[]{:S(2)}) async-start(), calls=%async_computation.11 | async-start | bytes 1216512 | tf_op jit(solution)/shard_map/all_gather | solution.py:137
  8.7 258.4 %reduce-scatter.15.cloned.1.call-start = ((), (), s32[]{:S(2)}) async-start(), calls=%async_computation.13 | async-start | bytes 7077888 | tf_op jit(solution)/shard_map/reduce_scatter | solution.py:217
  150.0 248.0 %all-gather.13.cloned.1.call-start = ((), (), s32[]{:S(2)}) async-start(), calls=%async_computation.12 | async-start | bytes 1216512 | tf_op jit(solution)/shard_map/all_gather | solution.py:135
  150.6 384.6 %all-gather.15.cloned.1.call-start = ((), (), s32[]{:S(2)}) async-start(), calls=%async_computation.14 | async-start | bytes 3538944 | tf_op jit(solution)/shard_map/all_gather | solution.py:220
  269.0 371.0 %all-gather.17.cloned.1.call-start = ((), (), s32[]{:S(2)}) async-start(), calls=%async_computation.15 | async-start | bytes 1216512 | tf_op jit(solution)/shard_map/all_gather | solution.py:138
  269.6 374.3 %all-gather.19.cloned.1.call-start = ((), (), s32[]{:S(2)}) async-start(), calls=%async_computation.16 | async-start | bytes 4866048 | tf_op jit(solution)/shard_map/all_gather | solution.py:139
  270.4 400.5 %all-gather.21.cloned.1.call-start = ((), (), s32[]{:S(2)}) async-start(), calls=%async_computation.17 | async-start | bytes 4866048 | tf_op jit(solution)/shard_map/all_gather | solution.py:140
  284.0 217.1 %all-to-all-start = ((bf16[8,3,64,1536]{3,2,1,0:T(8,128)(2,1)}), bf16[8,3,64,1536]{3,2,1,0:T(8,128)(2,1)}, u32[]{:S(2)}, u32[]{:S(2)}) async-start(bf16[8,3,64,1536]{3,2,1,0:T(8,128)(2,1)} %broadcast_select_fusion), calls=%async_computation.1 | async-start | bytes 9437184 | tf_op jit(solution)/shard_map/all_to_all | solution.py:245
  288.7 635.1 %reduce-scatter.17.cloned.1.call-start = ((), (), s32[]{:S(2)}) async-start(), calls=%async_computation.18 | async-start | bytes 7077888 | tf_op jit(solution)/shard_map/reduce_scatter | solution.py:540
  289.5 113.6 %collective-permute-start = (bf16[2,256,1536]{2,1,0:T(8,128)(2,1)S(1)}, bf16[2,256,1536]{2,1,0:T(8,128)(2,1)}, u32[]{:S(2)}, u32[]{:S(2)}) collective-permute-start(bf16[2,256,1536]{2,1,0:T(8,128)(2,1)S(1)} %bitcast.370), channel_id=1, source_target_pairs={{0,8},{4,12},{8,16},{12,20},{16,24},{20,28},{1,9},{5,13},{9,17},{1... | collective-permute-start | bytes 4718600 | tf_op jit(solution)/shard_map/ppermute | solution.py:20
  295.0 115.4 %collective-permute-start.1 = (bf16[2,256,1536]{2,1,0:T(8,128)(2,1)S(1)}, bf16[2,256,1536]{2,1,0:T(8,128)(2,1)}, u32[]{:S(2)}, u32[]{:S(2)}) collective-permute-start(bf16[2,256,1536]{2,1,0:T(8,128)(2,1)S(1)} %bitcast.371), channel_id=1, source_target_pairs={{0,4},{4,8},{8,12},{12,16},{16,20},{20,24},{24,28},{1,5},{5,9},{9,... | collective-permute-start | bytes 4718600 | tf_op jit(solution)/shard_map/ppermute | solution.py:20
  305.4 106.6 %collective-permute-start.2 = (bf16[2,256,1536]{2,1,0:T(8,128)(2,1)S(1)}, bf16[2,256,1536]{2,1,0:T(8,128)(2,1)}, u32[]{:S(2)}, u32[]{:S(2)}) collective-permute-start(bf16[2,256,1536]{2,1,0:T(8,128)(2,1)S(1)} %bitcast.372), channel_id=1, source_target_pairs={{4,0},{8,4},{12,8},{16,12},{20,16},{24,20},{28,24},{5,1},{9,5},{13... | collective-permute-start | bytes 4718600 | tf_op jit(solution)/shard_map/ppermute | solution.py:20
  307.6 158.5 %collective-permute-start.3 = (bf16[2,256,1536]{2,1,0:T(8,128)(2,1)S(1)}, bf16[2,256,1536]{2,1,0:T(8,128)(2,1)}, u32[]{:S(2)}, u32[]{:S(2)}) collective-permute-start(bf16[2,256,1536]{2,1,0:T(8,128)(2,1)S(1)} %bitcast.373), channel_id=1, source_target_pairs={{8,0},{12,4},{16,8},{20,12},{24,16},{28,20},{9,1},{13,5},{17,9},{2... | collective-permute-start | bytes 4718600 | tf_op jit(solution)/shard_map/ppermute | solution.py:20
  786.0 544.8 %all-gather.23.cloned.1.call-start = ((), (), s32[]{:S(2)}) async-start(), calls=%async_computation.19 | async-start | bytes 3538944 | tf_op jit(solution)/shard_map/all_gather | solution.py:544
  925.8 489.8 %reduce-scatter.19.cloned.1.call-start = ((), (), s32[]{:S(2)}) async-start(), calls=%async_computation.20 | async-start | bytes 2433024 | tf_op jit(solution)/shard_map/reduce_scatter | solution.py:597
  971.9 443.6 %reduce-scatter.25.cloned.1.call-start = ((), (), s32[]{:S(2)}) async-start(), calls=%async_computation.23 | async-start | bytes 2433024
  996.1 419.5 %reduce-scatter.21.cloned.1.call-start = ((), (), s32[]{:S(2)}) async-start(), calls=%async_computation.21 | async-start | bytes 9732096 | tf_op jit(solution)/shard_map/reduce_scatter | solution.py:598
  1114.1 193.2 %all-to-all-start.1 = ((bf16[8,3,64,1536]{3,2,1,0:T(8,128)(2,1)}), bf16[8,3,64,1536]{3,2,1,0:T(8,128)(2,1)}, u32[]{:S(2)}, u32[]{:S(2)}) async-start(bf16[8,3,64,1536]{3,2,1,0:T(8,128)(2,1)} %bitcast.394), calls=%async_computation.3 | async-start | bytes 9437184 | tf_op jit(solution)/shard_map/all_to_all | solution.py:567
  1118.9 425.5 %reduce-scatter.23.cloned.1.call-start = ((), (), s32[]{:S(2)}) async-start(), calls=%async_computation.22 | async-start | bytes 9732096 | tf_op jit(solution)/shard_map/reduce_scatter | solution.py:599
  1129.2 518.9 %reduce-scatter.27.cloned.1.call-start = ((), (), s32[]{:S(2)}) async-start(), calls=%async_computation.24 | async-start | bytes 2433024
  1205.5 79.2 %collective-permute-start.5 = (bf16[2,256,1536]{2,1,0:T(8,128)(2,1)}, bf16[2,256,1536]{2,1,0:T(8,128)(2,1)S(1)}, u32[]{:S(2)}, u32[]{:S(2)}) collective-permute-start(bf16[2,256,1536]{2,1,0:T(8,128)(2,1)} %get-tuple-element.191), channel_id=1, source_target_pairs={{0,4},{4,8},{8,12},{12,16},{16,20},{20,24},{24,28},{1,5},{5,9},{9,... | collective-permute-start | bytes 4718600 | tf_op jit(solution)/shard_map/ppermute | solution.py:20
  1210.9 73.8 %collective-permute-start.6 = (bf16[2,256,1536]{2,1,0:T(8,128)(2,1)}, bf16[2,256,1536]{2,1,0:T(8,128)(2,1)}, u32[]{:S(2)}, u32[]{:S(2)}) collective-permute-start(bf16[2,256,1536]{2,1,0:T(8,128)(2,1)} %get-tuple-element.192), channel_id=1, source_target_pairs={{4,0},{8,4},{12,8},{16,12},{20,16},{24,20},{28,24},{5,1},{9,5},{13... | collective-permute-start | bytes 4718600 | tf_op jit(solution)/shard_map/ppermute | solution.py:20
  1212.2 89.4 %collective-permute-start.7 = (bf16[2,256,1536]{2,1,0:T(8,128)(2,1)}, bf16[2,256,1536]{2,1,0:T(8,128)(2,1)}, u32[]{:S(2)}, u32[]{:S(2)}) collective-permute-start(bf16[2,256,1536]{2,1,0:T(8,128)(2,1)} %get-tuple-element.193), channel_id=1, source_target_pairs={{8,0},{12,4},{16,8},{20,12},{24,16},{28,20},{9,1},{13,5},{17,9},{2... | collective-permute-start | bytes 4718600 | tf_op jit(solution)/shard_map/ppermute | solution.py:20
  1356.8 395.9 %reduce-scatter.29.cloned.1.call-start = ((), (), s32[]{:S(2)}) async-start(), calls=%async_computation.25 | async-start | bytes 2433024
  (168 other events, 2813.1 us)
Sparse Core Ops, SparseCore 0:
  10.9 56.8 all-gather.8
  70.7 52.9 all-gather.10
  150.1 116.9 reduce-scatter.14
  269.9 128.0 all-gather.12
  400.6 85.2 all-gather.14
  488.6 51.3 all-gather.16
  542.9 62.5 all-gather.18
  608.4 62.4 all-gather.20
  786.1 137.6 reduce-scatter.16
  925.9 59.5 all-gather.22
  991.4 97.6 reduce-scatter.18
  1095.7 159.8 reduce-scatter.24
  1262.1 140.2 reduce-scatter.20
  1409.7 134.6 reduce-scatter.22
  1550.1 97.9 reduce-scatter.26
  1654.7 98.0 reduce-scatter.28
where the time goes:
time: 1770 us; the launch traced here: 1760 us
  waiting for transfers between devices  909 us (51%)
  local copies, waits for them, and re-layouts  294 us (17%)
  matrix products  246 us (14%)
  other arithmetic  179 us (10%)
  blocking collectives  82.5 us (5%)
  starting transfers between devices  32.4 us (2%)
    unnamed x19, waiting for transfers between devices  212 us
    ppermute x8, waiting for transfers between devices, shifted(): return lax.ppermute(x, axis, pairs)  146 us
    reduce_scatter x1, waiting for transfers between devices, on_device(): lax.psum_scatter(glob_grad.reshape(-1, kv_width), 'seq', scatter_dimensio...  138 us
    reduce_scatter x1, waiting for transfers between devices, on_device(): lax.psum_scatter(grad_down, ('seq', 'batch'), scatter_dimension=0, tiled=...  129 us
    reduce_scatter x1, waiting for transfers between devices, on_device(): lax.psum_scatter(glob_table, 'seq', scatter_dimension=0, tiled=True)  116 us
    all_gather x1, waiting for transfers between devices, on_device(): lax.all_gather(shards[0], ('seq', 'batch'), axis=0, tiled=True)  89.1 us
    unnamed x2, blocking collectives  82.5 us
    concatenate x8, local copies, waits for them, and re-layouts, on_device(): jnp.concatenate([rand_key_grad.reshape(blk_dev, RAND * BLK, model_width),...  56.2 us
  transfers between devices with their start and end apart: 26, of which 15 were waited for; matrix products, arithmetic and copies ran while one was open for 32% of the time, Pallas kernels for 0%

commit v1 on v0

v1 whole, which is shorter than its diff:
```python
import functools

import jax
import jax.numpy as jnp
from jax import lax
from jax.experimental import pallas as pl
from jax.experimental.pallas import tpu as pltpu
from jax.sharding import PartitionSpec as P

F32 = jnp.float32
BF = jnp.bfloat16

MESH = pl.DeviceIdType.MESH
PIECE = 592
ROWS = 304


def place():
    s, b = lax.axis_index("seq"), lax.axis_index("batch")
    return s // 2, s % 2, b // 2, b % 2


def device(z, x, y, c):
    return (2 * z + x, 2 * y + c)


def greet(z, x, y, c):
    barrier = pltpu.get_barrier_semaphore()

    def tell(to):
        pl.semaphore_signal(barrier, inc=1, device_id=to, device_id_type=MESH)

    tell(device(z, 1 - x, y, c))
    tell(device(z, x, 1 - y, c))
    tell(device(z, x, y, 1 - c))
    pl.when(z > 0)(lambda: tell(device(z - 1, x, y, c)))
    pl.when(z < 3)(lambda: tell(device(z + 1, x, y, c)))
    pl.semaphore_wait(barrier, 3 + (z > 0).astype(jnp.int32) + (z < 3).astype(jnp.int32))


def lanes(c):
    return pl.ds(pl.multiple_of(c * 384, 128), 384)


def remote(src, dst, send, recv, to):
    return pltpu.make_async_remote_copy(
        src_ref=src, dst_ref=dst, send_sem=send, recv_sem=recv, device_id=to, device_id_type=MESH
    )


def gather_kernel(x_ref, own_ref, xall, wall, mate, merged, mate_sem, local_sem,
                  wsend, wrecv, crecv, xsend, xrecv):
    z, x, y, c = place()
    UP, DOWN, XX, YY, CC = range(5)
    to = {
        UP: device(z + 1, x, y, c),
        DOWN: device(z - 1, x, y, c),
        XX: device(z, 1 - x, y, c),
        YY: device(z, x, 1 - y, c),
        CC: device(z, x, y, 1 - c),
    }
    can = {UP: z < 3, DOWN: z > 0, XX: None, YY: None, CC: None}
    mine, theirs = lanes(c), lanes(1 - c)

    def x_piece(zz, xx):
        return pl.ds(pl.multiple_of((2 * zz + xx) * 256, 256), 256)

    def x_copy(zz, xx, way, src=None):
        i = 2 * zz + xx
        ref = xall.at[:, x_piece(zz, xx), :]
        return remote(ref if src is None else src, ref, xsend.at[i, way], xrecv.at[i], to[way])

    def w_copy(zz, xx, yy, way, src=None):
        i = (2 * zz + xx) * 2 + yy
        ref = wall.at[i, :, mine]
        return remote(ref if src is None else src, ref, wsend.at[i, way],
                      crecv.at[i] if way == CC else wrecv.at[i], to[way])

    def guarded(way, act):
        if can[way] is None:
            act()
        else:
            pl.when(can[way])(act)

    greet(z, x, y, c)
    swap = remote(own_ref.at[:, theirs], mate, mate_sem.at[0], mate_sem.at[1], to[CC])
    swap.start()
    keep_x = pltpu.make_async_copy(x_ref, xall.at[:, x_piece(z, x), :], local_sem.at[0])
    keep_x.start()
    for way in (UP, DOWN, XX):
        guarded(way, lambda way=way: x_copy(z, x, way, x_ref).start())
    swap.wait()
    for seg in range(8):
        here = own_ref[24 * seg:24 * seg + 24, mine]
        there = mate[24 * seg:24 * seg + 24, :]
        pair = jnp.where(c == 0, jnp.concatenate([here, there], 0), jnp.concatenate([there, here], 0))
        merged[48 * seg:48 * seg + 48, :] = pair.astype(BF)
    here, there = own_ref[192:288, mine], mate[192:288, :]
    merged[384:576, :] = jnp.where(
        c == 0, jnp.concatenate([here, there], 0), jnp.concatenate([there, here], 0)
    ).astype(BF)
    merged[576:592, :] = (own_ref[288:304, mine] + mate[288:304, :]).astype(BF)
    keep_w = pltpu.make_async_copy(merged, wall.at[(2 * z + x) * 2 + y, :, mine], local_sem.at[1])
    keep_w.start()
    for way in (UP, DOWN, XX, YY, CC):
        guarded(way, lambda way=way: w_copy(z, x, y, way, merged).start())

    for k in range(1, 4):
        def from_below(k=k):
            x_copy(z - k, x, UP).wait_recv()
            pl.when(z < 3)(lambda: x_copy(z - k, x, UP).start())
            x_copy(z - k, x, XX).start()
            w_copy(z - k, x, y, UP).wait_recv()
            pl.when(z < 3)(lambda: w_copy(z - k, x, y, UP).start())
            for way in (XX, YY, CC):
                w_copy(z - k, x, y, way).start()

        def from_above(k=k):
            x_copy(z + k, x, DOWN).wait_recv()
            pl.when(z > 0)(lambda: x_copy(z + k, x, DOWN).start())
            x_copy(z + k, x, XX).start()
            w_copy(z + k, x, y, DOWN).wait_recv()
            pl.when(z > 0)(lambda: w_copy(z + k, x, y, DOWN).start())
            for way in (XX, YY, CC):
                w_copy(z + k, x, y, way).start()

        pl.when(z >= k)(from_below)
        pl.when(z + k <= 3)(from_above)

    def around(act):
        act(z)
        for k in range(1, 4):
            pl.when(z >= k)(lambda k=k: act(z - k))
            pl.when(z + k <= 3)(lambda k=k: act(z + k))

    def from_x(zz):
        w_copy(zz, 1 - x, y, XX).wait_recv()
        w_copy(zz, 1 - x, y, YY).start()
        w_copy(zz, 1 - x, y, CC).start()

    around(from_x)
    for xx in (x, 1 - x):
        def from_y(zz, xx=xx):
            w_copy(zz, xx, 1 - y, YY).wait_recv()
            w_copy(zz, xx, 1 - y, CC).start()

        around(from_y)
    around(lambda zz: x_copy(zz, 1 - x, XX).wait_recv())

    def from_mate(i, _):
        remote(wall.at[i, :, theirs], wall.at[i, :, theirs], wsend.at[i, CC], crecv.at[i], to[CC]).wait_recv()
        return 0

    lax.fori_loop(0, 16, from_mate, 0)
    keep_x.wait()
    keep_w.wait()
    for k in range(4):
        def z_line(zz, k=k):
            x_copy(zz, x, XX).wait_send()
            for way in (XX, YY, CC):
                w_copy(zz, x, y, way).wait_send()
            w_copy(zz, 1 - x, y, YY).wait_send()
            w_copy(zz, 1 - x, y, CC).wait_send()
            w_copy(zz, x, 1 - y, CC).wait_send()
            w_copy(zz, 1 - x, 1 - y, CC).wait_send()

        z_line(k)
        def ups(k=k):
            x_copy(k, x, UP).wait_send()
            w_copy(k, x, y, UP).wait_send()

        def downs(k=k):
            x_copy(k, x, DOWN).wait_send()
            w_copy(k, x, y, DOWN).wait_send()

        pl.when((k <= z) & (z < 3))(ups)
        pl.when((k >= z) & (z > 0))(downs)


def gather_all(x, own):
    dma = pltpu.SemaphoreType.DMA
    return pl.pallas_call(
        gather_kernel,
        out_shape=[
            jax.ShapeDtypeStruct((x.shape[0], 8 * x.shape[1], x.shape[2]), BF),
            jax.ShapeDtypeStruct((16, PIECE, 768), BF),
        ],
        in_specs=[pl.BlockSpec(memory_space=pl.ANY), pl.BlockSpec(memory_space=pltpu.VMEM)],
        out_specs=[pl.BlockSpec(memory_space=pl.ANY)] * 2,
        scratch_shapes=[
            pltpu.VMEM((ROWS, 384), F32), pltpu.VMEM((PIECE, 384), BF),
            dma((2,)), dma((2,)), dma((16, 5)), dma((16,)), dma((16,)), dma((8, 3)), dma((8,)),
        ],
        compiler_params=pltpu.CompilerParams(
            collective_id=0, has_side_effects=True, vmem_limit_bytes=48 * 2**20
        ),
    )(x, own)


def scatter_kernel(gq, gk, gv, go, gu, gd, gb, dxp, dxo_in,
                   oq, ok, ov, oo, ou, od, ob, odx,
                   acc, mate, yr, xr, zr, dacc, dxr, dzr, fin, snd, rcv, own_dx,
                   lsem, msend, mrecv, ysem, xsem, zsem, dlsem, dxsem, dzsem, fsem):
    z, x, y, c = place()
    mine, theirs = lanes(c), lanes(1 - c)
    near_x, near_y, near_c = device(z, 1 - x, y, c), device(z, x, 1 - y, c), device(z, x, y, 1 - c)
    above, below = device(z + 1, x, y, c), device(z - 1, x, y, c)

    def parts(yy, cc):
        off = pl.multiple_of(cc * 384, 128)
        for i, (ref, start, rows) in enumerate(
            ((gq, 0, 48), (gk, 48, 48), (gv, 96, 48), (go, 144, 48), (gd, 384, 192), (gb, 576, 16))
        ):
            yield i, ref.at[:, yy, :, pl.ds(off, 384)], pl.ds(start, rows)
        for j in range(4):
            col = pl.multiple_of(j * 768 + cc * 384, 128)
            yield 6 + j, gu.at[:, yy, :, pl.ds(col, 384)], pl.ds(192 + 48 * j, 48)

    def far(i):
        return jnp.where(z < 2, 3 - i, i)

    def dx_send(zz):
        return remote(dxp.at[:, pl.ds(pl.multiple_of((2 * zz + 1 - x) * 256, 256), 256), :], dxr.at[zz],
                      dxsem.at[0, zz], dxsem.at[1, zz], near_x)

    greet(z, x, y, c)
    for i in range(4):
        dx_send(far(i)).start()
    locals_, swaps = {}, {}
    for t, yy in enumerate((1 - y, y)):
        for i, src, rows in parts(yy, 1 - c):
            swaps[t, i] = remote(src, mate.at[:, yy, rows, :], msend.at[t, i], mrecv.at[t, i], near_c)
            swaps[t, i].start()
        for i, src, rows in parts(yy, c):
            locals_[t, i] = pltpu.make_async_copy(src, acc.at[:, yy, rows, :], lsem.at[t, i])
            locals_[t, i].start()
    dx_local = []
    for zz in range(4):
        cp = pltpu.make_async_copy(
            dxp.at[:, pl.ds(pl.multiple_of((2 * zz + x) * 256, 256), 256), :], dacc.at[zz], dlsem.at[zz])
        cp.start()
        dx_local.append(cp)
    own_cp = pltpu.make_async_copy(dxo_in, own_dx, dlsem.at[4])
    own_cp.start()

    def y_copy(s):
        return remote(acc.at[s, 1 - y], yr.at[s], ysem.at[0, s], ysem.at[1, s], near_y)

    def x_copy(zz):
        return remote(acc.at[2 * zz + 1 - x, y], xr.at[zz], xsem.at[0, zz], xsem.at[1, zz], near_x)

    def z_copy(zz, way):
        return remote(acc.at[2 * zz + x, y], zr.at[way, zz], zsem.at[0, way, zz], zsem.at[1, way, zz],
                      above if way == 0 else below)

    def dz_copy(zz, way):
        return remote(dacc.at[zz], dzr.at[way, zz], dzsem.at[0, way, zz], dzsem.at[1, way, zz],
                      above if way == 0 else below)

    for i in range(10):
        locals_[0, i].wait()
        swaps[0, i].wait_recv()

    def y_step(i, _):
        s = 2 * far(i % 4) + jnp.where(i < 4, 1 - x, x)
        acc[s, 1 - y] = (acc[s, 1 - y].astype(F32) + mate[s, 1 - y].astype(F32)).astype(BF)
        y_copy(s).start()
        return 0

    lax.fori_loop(0, 8, y_step, 0)
    for i in range(10):
        locals_[1, i].wait()
        swaps[1, i].wait_recv()

    def x_step(i, _):
        zz = far(i)
        s = 2 * zz + 1 - x
        y_copy(s).wait_recv()
        acc[s, y] = (acc[s, y].astype(F32) + mate[s, y].astype(F32) + yr[s].astype(F32)).astype(BF)
        x_copy(zz).start()
        return 0

    lax.fori_loop(0, 4, x_step, 0)
    for cp in dx_local:
        cp.wait()

    def z_step(zz, way, has_more):
        s = 2 * zz + x
        dx_send(zz).wait_recv()
        dacc[zz] = (dacc[zz].astype(F32) + dxr[zz].astype(F32)).astype(BF)

        def more_dx():
            dz_copy(zz, way).wait_recv()
            dacc[zz] = (dacc[zz].astype(F32) + dzr[way, zz].astype(F32)).astype(BF)

        pl.when(has_more)(more_dx)
        dz_copy(zz, way).start()
        y_copy(s).wait_recv()
        x_copy(zz).wait_recv()
        acc[s, y] = (acc[s, y].astype(F32) + mate[s, y].astype(F32) + yr[s].astype(F32)
                     + xr[zz].astype(F32)).astype(BF)

        def more():
            z_copy(zz, way).wait_recv()
            acc[s, y] = (acc[s, y].astype(F32) + zr[way, zz].astype(F32)).astype(BF)

        pl.when(has_more)(more)
        z_copy(zz, way).start()

    for i in range(3):
        pl.when(3 - i > z)(lambda i=i: z_step(3 - i, 0, z > 0))
        pl.when(i < z)(lambda i=i: z_step(i, 1, z < 3))
    s = 2 * z + x
    dx_send(z).wait_recv()
    own_cp.wait()
    odx[...] = own_dx[...] + dacc[z].astype(F32) + dxr[z].astype(F32)
    for way, cond in ((0, z > 0), (1, z < 3)):
        def last_dx(way=way):
            dz_copy(z, way).wait_recv()
            odx[...] += dzr[way, z].astype(F32)

        pl.when(cond)(last_dx)
    y_copy(s).wait_recv()
    x_copy(z).wait_recv()
    fin[...] = acc[s, y].astype(F32) + mate[s, y].astype(F32) + yr[s].astype(F32) + xr[z].astype(F32)
    for way, cond in ((0, z > 0), (1, z < 3)):
        def last(way=way):
            z_copy(z, way).wait_recv()
            fin[...] += zr[way, z].astype(F32)

        pl.when(cond)(last)

    def rows_of(cc):
        for seg in range(8):
            yield 24 * seg, pl.multiple_of(48 * seg + 24 * cc, 8), 24
        yield 192, pl.multiple_of(384 + 96 * cc, 8), 96
        yield 288, 576, 16

    for dst, src, n in rows_of(1 - c):
        snd[pl.ds(dst, n), :] = fin[pl.ds(src, n), :]
    last_swap = remote(snd, rcv, fsem.at[0], fsem.at[1], near_c)
    last_swap.start()
    outs = (oq, ok, ov, oo)

    def put(cols, get):
        for i, out in enumerate(outs):
            out[:, cols] = get(24 * i, 24)

    for (dst, src, n), slot in zip(rows_of(c), range(10)):
        value = fin[pl.ds(src, n), :]
        if slot < 4:
            outs[slot][:, mine] = value
        elif slot < 8:
            ou[:, pl.ds(pl.multiple_of((slot - 4) * 768 + c * 384, 128), 384)] = value
        elif slot == 8:
            od[:, mine] = value
        else:
            ob[:, mine] = value
    last_swap.wait()
    for (dst, src, n), slot in zip(rows_of(c), range(10)):
        value = rcv[pl.ds(dst, n), :]
        if slot < 4:
            outs[slot][:, theirs] = value
        elif slot < 8:
            ou[:, pl.ds(pl.multiple_of((slot - 4) * 768 + (1 - c) * 384, 128), 384)] = value
        elif slot == 8:
            od[:, theirs] = value
        else:
            ob[:, theirs] = value
    for i in range(10):
        swaps[0, i].wait_send()
        swaps[1, i].wait_send()
    for i in range(8):
        y_copy(i).wait_send()
    for i in range(4):
        x_copy(i).wait_send()
        dx_send(i).wait_send()

        def ups(i=i):
            z_copy(i, 0).wait_send()
            dz_copy(i, 0).wait_send()

        def downs(i=i):
            z_copy(i, 1).wait_send()
            dz_copy(i, 1).wait_send()

        pl.when(i > z)(ups)
        pl.when(i < z)(downs)


def scatter_all(gq, gk, gv, go, gu, gd, gb, dxp, own):
    dma = pltpu.SemaphoreType.DMA
    sd = jax.ShapeDtypeStruct
    views = [g.reshape(8, 2, 48, g.shape[-1]) for g in (gq, gk, gv, go, gu)]
    views += [gd.reshape(8, 2, 192, 768), jnp.broadcast_to(gb.astype(BF), (8, 2, 16, 768)), dxp, own]
    mb = own.shape[0]
    v = pltpu.VMEM
    return pl.pallas_call(
        scatter_kernel,
        out_shape=[sd((24, 768), F32)] * 4 + [sd((24, 3072), F32), sd((96, 768), F32), sd((16, 768), F32),
                                              sd(own.shape, F32)],
        in_specs=[pl.BlockSpec(memory_space=pl.ANY)] * 9,
        out_specs=[pl.BlockSpec(memory_space=pltpu.VMEM)] * 8,
        scratch_shapes=[
            v((8, 2, PIECE, 384), BF), v((8, 2, PIECE, 384), BF), v((8, PIECE, 384), BF), v((4, PIECE, 384), BF),
            v((2, 4, PIECE, 384), BF), v((4, mb, 256, 768), BF), v((4, mb, 256, 768), BF),
            v((2, 4, mb, 256, 768), BF), v((PIECE, 384), F32), v((ROWS, 384), F32), v((ROWS, 384), F32),
            v((mb, 256, 768), F32),
            dma((2, 10)), dma((2, 10)), dma((2, 10)), dma((2, 8)), dma((2, 4)), dma((2, 2, 4)), dma((5,)),
            dma((2, 4)), dma((2, 2, 4)), dma((2,)),
        ],
        compiler_params=pltpu.CompilerParams(
            collective_id=1, has_side_effects=True, vmem_limit_bytes=58 * 2**20
        ),
    )(*views)

NS = 2304
CHUNKS = 9


def dot(a, b):
    return lax.dot_general(a, b, (((1,), (0,)), ((), ())), preferred_element_type=F32)


def dot_nt(a, b):
    return lax.dot_general(a, b, (((1,), (1,)), ((), ())), preferred_element_type=F32)


def dot_tn(a, b):
    return lax.dot_general(a, b, (((0,), (0,)), ((), ())), preferred_element_type=F32)


def project_kernel(idx, xall, wall, bias, xs_ref, k_ref, v_ref, q_ref, xs, w, sems, wsem):
    m, i = pl.program_id(0), pl.program_id(1)

    @pl.when((m == 0) & (i == 0))
    def _():
        copy = pltpu.make_async_copy(wall.at[:, pl.ds(0, 144), :], w, wsem)
        copy.start()
        for mm in range(2):
            for cc in range(CHUNKS):
                pieces = [(0, 256)] if cc < 5 else [(0, 128), (128, 128)] if cc == 5 else [(64 * t, 64) for t in range(4)]
                base = cc if cc < 5 else 5 if cc == 5 else 7 + 4 * (cc - 6)
                for t, (off, n) in enumerate(pieces):
                    start = pl.multiple_of(idx[mm, base + t], 64)
                    pltpu.make_async_copy(xall.at[mm, pl.ds(start, n), :], xs.at[mm, cc, pl.ds(off, n), :],
                                          sems.at[mm, cc]).start()
        copy.wait()

    pltpu.make_async_copy(xall.at[0, pl.ds(0, 256), :], xs.at[m, i], sems.at[m, i]).wait()
    rows = xs[m, i]
    xs_ref[0] = rows
    k_ref[0] = dot(rows, w[:, 48:96, :].reshape(768, 768)).astype(BF)
    v_ref[0] = (dot(rows, w[:, 96:144, :].reshape(768, 768)) + bias[1:2, :]).astype(BF)

    @pl.when(i == 2)
    def _():
        q = (dot(rows, w[:, 0:48, :].reshape(768, 768)) + bias[0:1, :]).astype(BF)
        q_ref[0] = q * jnp.asarray(0.125, BF)


def project(idx, xall, wall, bias):
    mb = xall.shape[0]
    sd = jax.ShapeDtypeStruct
    chunk = pl.BlockSpec((1, 256, 768), lambda m, i, t: (m, i, 0))
    return pl.pallas_call(
        project_kernel,
        grid_spec=pltpu.PrefetchScalarGridSpec(
            num_scalar_prefetch=1,
            grid=(mb, CHUNKS),
            in_specs=[pl.BlockSpec(memory_space=pl.ANY)] * 2 + [pl.BlockSpec((16, 768), lambda m, i, t: (0, 0))],
            out_specs=[chunk, chunk, chunk, pl.BlockSpec((1, 256, 768), lambda m, i, t: (m, 0, 0))],
            scratch_shapes=[
                pltpu.VMEM((mb, CHUNKS, 256, 768), BF), pltpu.VMEM((16, 144, 768), BF),
                pltpu.SemaphoreType.DMA((mb, CHUNKS)), pltpu.SemaphoreType.DMA,
            ],
        ),
        out_shape=[sd((mb, NS, 768), BF)] * 3 + [sd((mb, 256, 768), BF)],
        compiler_params=pltpu.CompilerParams(vmem_limit_bytes=48 * 2**20),
    )(idx, xall, wall, bias)


EPS = 1e-6
G0, G1 = 0.7978845608, 0.044715


def norm(v):
    mean = jnp.mean(v, axis=-1, keepdims=True)
    centred = v - mean
    inverse = lax.rsqrt(jnp.mean(centred * centred, axis=-1, keepdims=True) + EPS)
    return centred * inverse, inverse


def norm_back(g, normed, inverse, gain):
    c = g * gain
    return inverse * (c - jnp.mean(c, axis=-1, keepdims=True)
                      - normed * jnp.mean(c * normed, axis=-1, keepdims=True))


def middle_kernel(att, x, cot, wall, bias, out_ref, datt_ref, done_ref, go_ref, gu_ref, gd_ref, gb_ref,
                  w, wsem, pre, hid, mid, low, n1, r1, ffn):
    rows = x.shape[0]
    copies = [
        pltpu.make_async_copy(wall.at[:, pl.ds(144, 48), :], w.at[:, pl.ds(0, 48), :], wsem.at[0]),
        pltpu.make_async_copy(wall.at[:, pl.ds(192, 192), :], w.at[:, pl.ds(48, 192), :], wsem.at[1]),
        pltpu.make_async_copy(wall.at[:, pl.ds(384, 192), :], w.at[:, pl.ds(240, 192), :], wsem.at[2]),
    ]
    for cp in copies:
        cp.start()
    half = rows // 2
    copies[0].wait()
    w_out = w[:, 0:48, :].reshape(768, 768)
    for h in range(2):
        r = pl.ds(h * half, half)
        t = x[r, :].astype(F32) + dot(att[r, :], w_out) + bias[2:3, :]
        normed, inverse = norm(t)
        n1[r, :] = normed
        r1[r, :] = jnp.broadcast_to(inverse, (half, 128))
        value = normed * bias[4:5, :] + bias[5:6, :]
        mid[r, :] = value
        low[r, :] = value.astype(BF)
    ffn[...] = jnp.broadcast_to(bias[3:4, :], ffn.shape)
    copies[1].wait()
    copies[2].wait()

    def up_block(j):
        return w[:, pl.ds(pl.multiple_of(48 + 48 * j, 16), 48), :].reshape(768, 768)

    def down_block(j):
        return w[pl.ds(4 * j, 4), 240:432, :].reshape(768, 768)

    def forward(j, _):
        wu, wd = up_block(j), down_block(j)
        for h in range(2):
            r = pl.ds(h * half, half)
            u = dot(low[r, :], wu) + bias[pl.ds(8 + j, 1), :]
            pre[j, r, :] = u
            g = (0.5 * u * (1.0 + jnp.tanh(G0 * (u + G1 * u * u * u)))).astype(BF)
            hid[j, r, :] = g
            ffn[r, :] += dot(g, wd)
        return 0

    lax.fori_loop(0, 4, forward, 0)
    gb_ref[...] = jnp.zeros_like(gb_ref)
    for h in range(2):
        r = pl.ds(h * half, half)
        normed, inverse = norm(mid[r, :] + ffn[r, :])
        out_ref[r, :] = (normed * bias[6:7, :] + bias[7:8, :]).astype(BF)
        g = cot[r, :].astype(F32)
        gb_ref[6:7, :] += jnp.sum(g * normed, axis=0, keepdims=True)
        gb_ref[7:8, :] += jnp.sum(g, axis=0, keepdims=True)
        d_two = norm_back(g, normed, inverse, bias[6:7, :])
        mid[r, :] = d_two
        d_ffn = d_two.astype(BF)
        datt_ref[r, :] = d_ffn
        gb_ref[3:4, :] += jnp.sum(d_ffn.astype(F32), axis=0, keepdims=True)

    def backward(j, _):
        wu, wd = up_block(j), down_block(j)
        d_ffn = datt_ref[...]
        gd_ref[pl.ds(pl.multiple_of(j * 768, 768), 768), :] = dot_tn(hid[j], d_ffn).astype(BF)
        for h in range(2):
            r = pl.ds(h * half, half)
            u = pre[j, r, :]
            th = jnp.tanh(G0 * (u + G1 * u * u * u))
            slope = 0.5 * (1.0 + th) + 0.5 * u * (1.0 - th * th) * (G0 * (1.0 + 3.0 * G1 * u * u))
            d_pre = (dot_nt(datt_ref[r, :], wd) * slope).astype(BF)
            hid[j, r, :] = d_pre
            gb_ref[pl.ds(8 + j, 1), :] += jnp.sum(d_pre.astype(F32), axis=0, keepdims=True)
            mid[r, :] += dot_nt(d_pre, wu)
        gu_ref[:, pl.ds(pl.multiple_of(j * 768, 768), 768)] = dot_tn(low[...], hid[j]).astype(BF)
        return 0

    lax.fori_loop(0, 4, backward, 0)
    for h in range(2):
        r = pl.ds(h * half, half)
        d_mid, normed = mid[r, :], n1[r, :]
        gb_ref[4:5, :] += jnp.sum(d_mid * normed, axis=0, keepdims=True)
        gb_ref[5:6, :] += jnp.sum(d_mid, axis=0, keepdims=True)
        d_one = norm_back(d_mid, normed, r1[r, 0:1], bias[4:5, :])
        done_ref[r, :] = d_one
        d_branch = d_one.astype(BF)
        low[r, :] = d_branch
        gb_ref[2:3, :] += jnp.sum(d_branch.astype(F32), axis=0, keepdims=True)
        datt_ref[r, :] = dot_nt(d_branch, w_out).astype(BF)
    go_ref[...] = dot_tn(att[...], low[...]).astype(BF)


def middle(att, x, cot, wall, bias):
    rows = x.shape[0]
    sd = jax.ShapeDtypeStruct
    vm = pl.BlockSpec(memory_space=pltpu.VMEM)
    return pl.pallas_call(
        middle_kernel,
        in_specs=[vm, vm, vm, pl.BlockSpec(memory_space=pl.ANY), vm],
        out_specs=[vm] * 7,
        out_shape=[sd((rows, 768), BF), sd((rows, 768), BF), sd((rows, 768), F32), sd((768, 768), BF),
                   sd((768, 3072), BF), sd((3072, 768), BF), sd((16, 768), F32)],
        scratch_shapes=[
            pltpu.VMEM((16, 432, 768), BF), pltpu.SemaphoreType.DMA((3,)),
            pltpu.VMEM((4, rows, 768), F32), pltpu.VMEM((4, rows, 768), BF),
            pltpu.VMEM((rows, 768), F32), pltpu.VMEM((rows, 768), BF), pltpu.VMEM((rows, 768), F32),
            pltpu.VMEM((rows, 128), F32), pltpu.VMEM((rows, 768), F32),
        ],
        compiler_params=pltpu.CompilerParams(vmem_limit_bytes=60 * 2**20),
    )(att, x, cot, wall, bias)


def back_kernel(scattered, idx, xs_ref, dk_ref, dv_ref, dq_ref, done_ref, wall, gb_in, dx_ref, own_ref, gq_ref, gk_ref, gv_ref, gb_ref,
                w, wsem, acc, aq, ak, av):
    m, i = pl.program_id(0), pl.program_id(1)

    @pl.when((m == 0) & (i == 0))
    def _():
        copy = pltpu.make_async_copy(wall.at[:, pl.ds(0, 144), :], w, wsem)
        copy.start()
        acc[...] = jnp.zeros_like(acc)
        aq[...] = jnp.zeros_like(aq)
        ak[...] = jnp.zeros_like(ak)
        av[...] = jnp.zeros_like(av)
        gb_ref[...] = gb_in[...]
        copy.wait()

    rows, dk, dv = xs_ref[0], dk_ref[0], dv_ref[0]
    ak[...] += dot_tn(rows, dk)
    av[...] += dot_tn(rows, dv)
    gb_ref[1:2, :] += jnp.sum(dv.astype(F32), axis=0, keepdims=True)
    dx = dot_nt(dk, w[:, 48:96, :].reshape(768, 768)) + dot_nt(dv, w[:, 96:144, :].reshape(768, 768))

    def add(slot, off, n):
        start = pl.multiple_of(idx[m, slot], 64)
        acc[m, pl.ds(start, n), :] += dx[off:off + n]

    if not scattered:
        dx_ref[0] = jnp.where(i == 2, jnp.zeros_like(dx), dx).astype(BF)

    @pl.when((i < 5) & (i != 2) & scattered)
    def _():
        add(jnp.minimum(i, 4), 0, 256)

    @pl.when((i == 5) & scattered)
    def _():
        add(5, 0, 128)
        add(6, 128, 128)

    @pl.when((i > 5) & scattered)
    def _():
        for t in range(4):
            add(7 + 4 * (i - 6) + t, 64 * t, 64)

    @pl.when(i == 2)
    def _():
        dq = dq_ref[0]
        aq[...] += dot_tn(rows, dq)
        gb_ref[0:1, :] += jnp.sum(dq.astype(F32), axis=0, keepdims=True)
        own_ref[0] = dx + done_ref[0] + dot_nt(dq, w[:, 0:48, :].reshape(768, 768))

    @pl.when((i == CHUNKS - 1) & scattered)
    def _():
        dx_ref[m if scattered else 0] = acc[m].astype(BF)

    @pl.when((m == 1) & (i == CHUNKS - 1))
    def _():
        gq_ref[...] = aq[...].astype(BF)
        gk_ref[...] = ak[...].astype(BF)
        gv_ref[...] = av[...].astype(BF)


def back(idx, xs, dk, dv, dq, done, wall, gb, seq_len):
    mb = xs.shape[0]
    sd = jax.ShapeDtypeStruct
    chunk = pl.BlockSpec((1, 256, 768), lambda m, i, t: (m, i, 0))
    one = pl.BlockSpec((1, 256, 768), lambda m, i, t: (m, 0, 0))
    whole = lambda *s: pl.BlockSpec(s, lambda m, i, t: (0,) * len(s))
    scattered = seq_len > 0
    held = seq_len if scattered else 256
    return pl.pallas_call(
        functools.partial(back_kernel, scattered),
        grid_spec=pltpu.PrefetchScalarGridSpec(
            num_scalar_prefetch=1,
            grid=(mb, CHUNKS),
            in_specs=[chunk, chunk, chunk, one, one, pl.BlockSpec(memory_space=pl.ANY), whole(16, 768)],
            out_specs=[whole(mb, seq_len, 768) if scattered else chunk, one, whole(768, 768), whole(768, 768), whole(768, 768), whole(16, 768)],
            scratch_shapes=[
                pltpu.VMEM((16, 144, 768), BF), pltpu.SemaphoreType.DMA, pltpu.VMEM((mb, held, 768), F32),
                pltpu.VMEM((768, 768), F32), pltpu.VMEM((768, 768), F32), pltpu.VMEM((768, 768), F32),
            ],
        ),
        out_shape=[sd((mb, seq_len if scattered else NS, 768), BF), sd((mb, 256, 768), F32), sd((768, 768), BF), sd((768, 768), BF),
                   sd((768, 768), BF), sd((16, 768), F32)],
        compiler_params=pltpu.CompilerParams(vmem_limit_bytes=60 * 2**20),
    )(idx, xs, dk, dv, dq, done, wall, gb)
HALF=128; WK=1152; NW=1280; NK=1664; NS=2304
def key_rows(h):
    return ((HALF*h,WK),(NW+HALF*h,HALF),(NW+2*HALF+384*h,384))
def cat_rows(ref,h):
    return jnp.concatenate([ref[0,pl.ds(a,n),:] for a,n in key_rows(h)],axis=0)
def split_heads(v):
    lane=lax.broadcasted_iota(jnp.int32,v.shape,1)
    z=jnp.zeros_like(v)
    return jnp.concatenate([jnp.where(lane<64,v,z),jnp.where(lane>=64,v,z)],axis=0)
def merge_heads(v):
    n=v.shape[0]//2
    lane=lax.broadcasted_iota(jnp.int32,(n,v.shape[1]),1)
    return jnp.where(lane<64,v[:n],v[n:])
def ind_ext(n):
    r=lax.broadcasted_iota(jnp.int32,(2*n,128),0); l=lax.broadcasted_iota(jnp.int32,(2*n,128),1)
    first=(r%n)<64
    return jnp.where(((l==0)&first)|((l==1)&jnp.logical_not(first)),1.0,0.0)
def ext3(base,col):
    l=lax.broadcasted_iota(jnp.int32,base.shape,1)
    hi=col.astype(BF).astype(F32); r=col-hi; mi=r.astype(BF).astype(F32); lo=r-mi
    return jnp.where(l==2,hi,jnp.where(l==3,mi,jnp.where(l==4,lo,base))).astype(BF)
def fwd_kernel(q_ref,k_ref,v_ref,me_ref,o_ref,l_ref):
    p=pl.program_id(1)
    ind=ind_ext(HALF).astype(BF)
    for h in range(2):
        me=me_ref[0,h]
        qe=jnp.concatenate([split_heads(q_ref[0,pl.ds(h*HALF,HALF),:]),ind],axis=1)
        ke=jnp.concatenate([cat_rows(k_ref,h),me],axis=1)
        s=dot_nt(qe,ke)
        top=jnp.max(s,axis=1,keepdims=True)
        e=jnp.exp(s-top).astype(BF)
        ve=jnp.concatenate([cat_rows(v_ref,h),me],axis=1)
        o=dot(e,ve)
        tot=o[:,130:131]
        o_ref[0,pl.ds(h*HALF,HALF),:]=merge_heads(o[:,:128]/tot).astype(BF)
        l_ref[0,0,pl.ds(h*256,256),:]=jnp.broadcast_to(top+jnp.log(tot),(256,128))
def attn_fwd(q,k,v,me):
    mb=q.shape[0]; npair=q.shape[2]//128
    return pl.pallas_call(fwd_kernel,grid=(mb,npair),
      in_specs=[pl.BlockSpec((1,256,128),lambda m,p:(m,0,p)),pl.BlockSpec((1,NS,128),lambda m,p:(m,0,p)),pl.BlockSpec((1,NS,128),lambda m,p:(m,0,p)),
        pl.BlockSpec((1,2,NK,128),lambda m,p:(m,0,0,0))],
      out_specs=[pl.BlockSpec((1,256,128),lambda m,p:(m,0,p)),pl.BlockSpec((1,1,512,128),lambda m,p:(m,p,0,0))],
      out_shape=[jax.ShapeDtypeStruct(q.shape,BF),jax.ShapeDtypeStruct((mb,npair,512,128),F32)],
      compiler_params=pltpu.CompilerParams(vmem_limit_bytes=56*2**20))(q,k,v,me)
def bwd_kernel(CH,q_ref,k_ref,v_ref,me_ref,o_ref,do_ref,l_ref,dq_ref,dk_ref,dv_ref,dka,dva):
    ind=ind_ext(HALF)
    zero=jnp.zeros_like(ind)
    dka[...]=jnp.zeros_like(dka); dva[...]=jnp.zeros_like(dva)
    for h in range(2):
        rows=pl.ds(h*HALF,HALF)
        qs=split_heads(q_ref[0,rows,:])
        do2=do_ref[0,rows,:]
        dos=split_heads(do2)
        o2=o_ref[0,rows,:].astype(F32)
        delta=jnp.sum(dos.astype(F32)*jnp.concatenate([o2,o2],axis=0),axis=1,keepdims=True)
        lse=l_ref[0,0,pl.ds(h*256,256),0:1]
        qe=jnp.concatenate([qs,ext3(ind,-lse)],axis=1)
        doe=jnp.concatenate([dos,ext3(zero,-delta)],axis=1)
        dqt=jnp.zeros((128,256),F32)
        off=0
        for a,n in key_rows(h):
            c0=0
            while c0<n:
                c=min(CH,n-c0)
                kr=pl.ds(a+c0,c)
                k2=k_ref[0,kr,:]; v2=v_ref[0,kr,:]; me=me_ref[0,h,pl.ds(off+c0,c),:]
                st=dot_nt(jnp.concatenate([k2,me],axis=1),qe)
                pt=jnp.exp(st)
                dpt=dot_nt(jnp.concatenate([v2,me],axis=1),doe)
                ds=(pt*dpt).astype(BF)
                dva[kr,:]+=dot(pt.astype(BF),dos)
                dka[kr,:]+=dot(ds,qs)
                dqt=dqt+dot(k2.T,ds)
                c0+=c
            off+=n
        dq_ref[0,rows,:]=(merge_heads(dqt.T)*0.125).astype(BF)
    dk_ref[0]=dka[...].astype(BF); dv_ref[0]=dva[...].astype(BF)
def attn_bwd(q,k,v,me,o,do,l,CH=384):
    mb=q.shape[0]; npair=q.shape[2]//128
    qs=pl.BlockSpec((1,256,128),lambda m,p:(m,0,p)); ks=pl.BlockSpec((1,NS,128),lambda m,p:(m,0,p))
    return pl.pallas_call(functools.partial(bwd_kernel,CH),grid=(mb,npair),
      in_specs=[qs,ks,ks,pl.BlockSpec((1,2,NK,128),lambda m,p:(m,0,0,0)),qs,qs,pl.BlockSpec((1,1,512,128),lambda m,p:(m,p,0,0))],
      out_specs=[qs,ks,ks],
      out_shape=[jax.ShapeDtypeStruct(q.shape,BF),jax.ShapeDtypeStruct(k.shape,BF),jax.ShapeDtypeStruct(k.shape,BF)],
      scratch_shapes=[pltpu.VMEM((NS,128),F32)]*2,
      compiler_params=pltpu.CompilerParams(vmem_limit_bytes=56*2**20))(q,k,v,me,o,do,l)


BLK = 64
WIN = 8
RAND = 3
ALL = ("seq", "batch")


def own_rows(wq, wk, wv, wo, wu, wd, vectors, b_up, owner, owners):
    width = wq.shape[1]
    lane = jnp.arange(width, dtype=jnp.int32)
    n = vectors[0].shape[0]
    table = jnp.stack(vectors).astype(F32)
    table = jnp.where(lane // n == owner, jnp.tile(table, (1, width // n)), 0.0)
    m = b_up.shape[0]
    flat = jnp.arange(4 * width, dtype=jnp.int32)
    ups = jnp.where(flat // m == owner, jnp.tile(b_up.astype(F32), 4 * width // m), 0.0).reshape(4, width)
    up = wu.reshape(wu.shape[0], 4, width).transpose(1, 0, 2).reshape(-1, width)
    rows = jnp.concatenate([wq, wk, wv, wo, up, wd], axis=0).astype(F32)
    return rows, jnp.concatenate([table, ups, jnp.zeros((4, width), F32)], axis=0)


def block_plan(lengths, randoms, device, blocks):
    ends = jnp.cumsum(lengths, axis=1)
    starts = ends - lengths

    def doc_of(block):
        at = block * BLK
        shape = (lengths.shape[0],) + (1,) * (block.ndim - 1) + (lengths.shape[1],)
        doc = jnp.sum((ends.reshape(shape) <= at[..., None]).astype(jnp.int32), axis=-1)
        doc = jnp.minimum(doc, lengths.shape[1] - 1)
        hit = jnp.arange(lengths.shape[1], dtype=jnp.int32) == doc[..., None]
        return doc, jnp.sum(jnp.where(hit, starts.reshape(shape), 0), axis=-1)

    mb = lengths.shape[0]
    half = jnp.arange(2, dtype=jnp.int32)
    query = device * 4 + 2 * half[:, None] + half[None, :]
    query = jnp.broadcast_to(query[None], (mb, 2, 2))
    q_doc, q_first = doc_of(query)
    window = device * 4 + 2 * half[:, None] - WIN + jnp.arange(2 * WIN + 2, dtype=jnp.int32)[None, :]
    window = jnp.broadcast_to(window[None], (mb, 2, 2 * WIN + 2))
    w_doc, w_first = doc_of(jnp.clip(window, 0, blocks - 1))
    w_good = (window >= 0) & (window < blocks) & (window * BLK - w_first >= 2 * BLK)
    see_window = (
        w_good[:, :, None, :]
        & (w_doc[:, :, None, :] == q_doc[..., None])
        & (jnp.abs(window[:, :, None, :] - query[..., None]) <= WIN)
    )
    see_glob = jnp.ones((mb, 2, 2, 2), bool)
    named = lax.dynamic_slice_in_dim(randoms, device * 4, 4, 1).reshape(mb, 2, 2, RAND)
    r_doc, r_first = doc_of(named)
    r_good = (
        (r_doc == q_doc[..., None])
        & (jnp.abs(named - query[..., None]) > WIN)
        & (named * BLK - r_first >= 2 * BLK)
    )
    see_random = (r_good[:, :, None] & jnp.eye(2, dtype=bool)[None, None, :, :, None]).reshape(mb, 2, 2, 2 * RAND)
    see = jnp.concatenate([see_window, see_glob, see_random], axis=3)
    bias = jnp.where(see, 0.0, -1e30).astype(BF)
    bias = jnp.broadcast_to(bias[..., None], bias.shape + (BLK,)).reshape(mb, 2, 2, -1, 1)
    lane = jnp.arange(128, dtype=jnp.int32)
    extra = jnp.where(
        lane == 0, bias[:, :, 0], jnp.where(lane == 1, bias[:, :, 1], jnp.where(lane < 5, 1.0, 0.0).astype(BF))
    )
    chunk = jnp.clip(device + jnp.arange(-2, 3, dtype=jnp.int32), 0, blocks // 4 - 1) * (4 * BLK)
    where = jnp.concatenate(
        [jnp.broadcast_to(chunk[None], (mb, 5)), q_first[:, :, 0], named.reshape(mb, -1) * BLK], axis=1
    )
    return where.astype(jnp.int32), extra


def on_device(inputs, cotangent, doc_lengths, random_blocks, wq, wk, wv, wo, wu, wd, b_query, b_value, b_out,
              b_up, b_down, gain_attn, bias_attn, gain_ffn, bias_ffn):
    mb, _, rows, width = inputs.shape
    devices, owners = lax.axis_size("seq"), lax.axis_size("seq") * lax.axis_size("batch")
    device = lax.axis_index("seq")
    owner = device * lax.axis_size("batch") + lax.axis_index("batch")
    linked = devices == 8 and owners == 32
    seq_len = devices * rows
    x, cot = inputs[:, 0], cotangent[:, 0]
    where, extra = block_plan(doc_lengths[:, 0], random_blocks[:, 0], device, seq_len // BLK)
    vectors = (b_query, b_value, b_out, b_down, gain_attn, bias_attn, gain_ffn, bias_ffn)
    packed, table = own_rows(wq, wk, wv, wo, wu, wd, vectors, b_up, owner, owners)
    if linked:
        xall, wall = gather_all(x, jnp.concatenate([packed, table], axis=0))
        bias = jnp.sum(wall[:, 576:592, :].astype(F32), axis=0)
    else:
        xall = lax.all_gather(x, "seq", axis=1, tiled=True)
        bias = lax.psum(table, ALL)
        full = [lax.all_gather(w, ALL, axis=0, tiled=True) for w in (wq, wk, wv, wo, wu, wd)]
        up = full[4].reshape(16, 48, 4, width).transpose(0, 2, 1, 3).reshape(16, 192, width)
        wall = jnp.concatenate(
            [w.reshape(16, 48, width) for w in full[:4]] + [up, full[5].reshape(16, 192, width),
                                                           jnp.zeros((16, 16, width), BF)], axis=1)
    xs, k, v, q = project(where, xall, wall, bias)
    att, lse = attn_fwd(q, k, v, extra)
    flat = lambda t: t.reshape(-1, t.shape[-1])
    out, datt, done, go, gu, gd, gb = middle(flat(att), flat(x), flat(cot), wall, bias)
    dq, dk, dv = attn_bwd(q, k, v, extra, att, datt.reshape(att.shape), lse, 640)
    done = done.reshape(mb, rows, width)
    if linked:
        dxp, own, gq, gk, gv, gb = back(where, xs, dk, dv, dq, done, wall, gb, seq_len)
        *grads, gb, dx = scatter_all(gq, gk, gv, go, gu, gd, gb, dxp, own)
    else:
        dxs, own, gq, gk, gv, gb = back(where, xs, dk, dv, dq, done, wall, gb, 0)
        start = jnp.concatenate([where[:, :5, None] + jnp.arange(0, 256, BLK), ], axis=1).reshape(mb, -1)
        glob = (where[:, 5:7, None] + jnp.arange(0, 128, BLK)).reshape(mb, -1)
        to = jnp.concatenate([start, glob, where[:, 7:]], axis=1) // BLK
        parts = dxs.reshape(mb, -1, BLK, width)
        total = jnp.zeros((mb, seq_len // BLK, BLK, width), F32)
        total = jax.vmap(lambda t, i, p: t.at[i].add(p))(total, to, parts.astype(F32))
        dx = own + lax.psum_scatter(total.reshape(mb, seq_len, width), "seq", scatter_dimension=1, tiled=True)
        grads = [lax.psum_scatter(g.astype(F32), ALL, scatter_dimension=0, tiled=True) for g in (gq, gk, gv, go, gu, gd)]
        gb = lax.psum(gb, ALL)
    n, m = b_query.shape[0], b_up.shape[0]
    small = lax.dynamic_slice_in_dim(gb[:8], owner * n, n, 1)
    ups = lax.dynamic_slice_in_dim(gb[8:12].reshape(-1), owner * m, m, 0)
    return (
        out.reshape(inputs.shape), dx[:, None], *grads,
        small[0], small[1], small[2], ups, small[3], small[4], small[5], small[6], small[7],
    )


def solution(mesh):
    tokens = P(None, "batch", "seq", None)
    mat, vec = P(ALL, None), P(ALL)
    in_specs = (tokens, tokens, P(None, "batch", None), P(None, "batch", None, None)) + (mat,) * 6 + (vec,) * 9
    out_specs = (tokens, tokens) + (mat,) * 6 + (vec,) * 9
    return jax.shard_map(on_device, mesh=mesh, in_specs=in_specs, out_specs=out_specs, check_vma=False)
```

time: 1770 us -> 500 us (0.28)
  waiting for transfers between devices: 909 us -> 0 us
  Pallas kernels: 0 us -> 460 us
  local copies, waits for them, and re-layouts: 294 us -> 19.6 us
  matrix products: 246 us -> 0 us
  other arithmetic: 179 us -> 9.84 us
  blocking collectives: 82.5 us -> 0 us
  starting transfers between devices: 32.4 us -> 0 us
    pallas_call x0 -> x7, Pallas kernels: none -> 460 us  [the longest x1 162 us: scatter_all(): pl.pallas_call(scatter_kernel, out_shape=[sd((24, 768), F32)] * 4 + [sd((...]
    reduce_scatter x5 -> x0, waiting for transfers between devices: 383 us -> none  [the longest x1 138 us: on_device(): lax.psum_scatter(glob_grad.reshape(-1, kv_width), 'seq', scatter_dimensio...]
    dot_general x54 -> x0, matrix products: 246 us -> none  [the longest x6 29.7 us: outer_sum(): lax.dot_general(left, right, (((0,), (0,)), ((), ())), preferred_element_...]
    unnamed x19 -> x0, waiting for transfers between devices: 212 us -> none
    all_gather x8 -> x0, waiting for transfers between devices: 168 us -> none  [the longest x1 89.1 us: on_device(): lax.all_gather(shards[0], ('seq', 'batch'), axis=0, tiled=True)]
    ppermute x8 -> x0, waiting for transfers between devices: 146 us -> none  [shifted(): return lax.ppermute(x, axis, pairs)]
    unnamed x2 -> x0, blocking collectives: 82.5 us -> none
    concatenate x9 -> x4, local copies, waits for them, and re-layouts: 57.7 us -> 1.08 us  [the longest x1 0.99 us: own_rows(): rows = jnp.concatenate([wq, wk, wv, wo, up, wd], axis=0).astype(F32)]
  transfers between devices with their start and end apart: 26 -> 0, of which waited for: 15 -> 0; matrix products, arithmetic and copies ran while one was open for 32% -> 0% of each run, Pallas kernels for 0% -> 0%
where the time goes in v1:
time: 500 us; the launch traced here: 491 us
  Pallas kernels  460 us (92%)
  local copies, waits for them, and re-layouts  19.6 us (4%)
  other arithmetic  9.84 us (2%)
    pallas_call x1, Pallas kernels, scatter_all(): pl.pallas_call(scatter_kernel, out_shape=[sd((24, 768), F32)] * 4 + [sd((...  162 us
    pallas_call x1, Pallas kernels, gather_all(): pl.pallas_call(gather_kernel, out_shape=[jax.ShapeDtypeStruct((x.shape[0]...  138 us
    pallas_call x1, Pallas kernels, back(): pl.pallas_call(functools.partial(back_kernel, scattered), grid_spec=pltpu...  39.9 us
    pallas_call x1, Pallas kernels, attn_bwd(): pl.pallas_call(functools.partial(bwd_kernel, CH), grid=(mb, npair), in_sp...  38.3 us
    pallas_call x1, Pallas kernels, middle(): pl.pallas_call(middle_kernel, in_specs=[vm, vm, vm, pl.BlockSpec(memory_s...  33.4 us
    pallas_call x1, Pallas kernels, attn_fwd(): pl.pallas_call(fwd_kernel, grid=(mb, npair), in_specs=[pl.BlockSpec((1, 2...  25.4 us
    pallas_call x1, Pallas kernels, project(): pl.pallas_call(project_kernel, grid_spec=pltpu.PrefetchScalarGridSpec(num...  23.5 us
    unnamed x34, local copies, waits for them, and re-layouts  10.8 us

profile of v1, /device:TPU:0, one launch (start us, length us, event | category | flops | bytes accessed | tf_op | source)
XLA Modules:
  0.0 490.8 jit_solution(14700209532061968407)
XLA Ops:
  0.7 0.8 broadcast_multiply_fusion
  1.6 0.9 reduce_window_sum.11
  4.7 0.8 stack.35
  5.7 0.8 constant_dynamic-update-slice_fusion.5
  6.4 0.8 constant_dynamic-update-slice_fusion.4
  7.2 0.8 constant_dynamic-update-slice_fusion.3
  8.0 0.8 constant_dynamic-update-slice_fusion.2
  8.7 0.9 copy.80
  9.7 1.0 constant_dynamic-update-slice_fusion
  10.9 138.4 %shard_map.314 = (bf16[2,2048,768]{2,1,0:T(8,128)(2,1)}, bf16[16,592,768]{2,1,0:T(8,128)(2,1)}) custom-call(bf16[2,256,768]{2,1,0:T(8,128)(2,1)S(1)} %bitcast.62, f32[304,768]{1,0:T(8,128)S(1)} %pad_maximum_fusion.own_ref), custom_call_target="tpu_custom_call" | custom-call | tf_op jit(solution)/shard_map/pallas_call | solution.py:182
  149.3 1.1 convert_reduce_fusion.bias
  150.4 23.5 %shard_map.315 = (bf16[2,2304,768]{2,1,0:T(8,128)(2,1)}, bf16[2,2304,768]{2,1,0:T(8,128)(2,1)}, bf16[2,2304,768]{2,1,0:T(8,128)(2,1)}, bf16[2,256,768]{2,1,0:T(8,128)(2,1)S(1)}) custom-call(s32[2,19]{1,0:T(2,128)S(1)} %pad_add_fusion.idx, bf16[2,2048,768]{2,1,0:T(8,128)(2,1)} %get-tuple-element.49.xall, bf16[16,592,768]{2,1,0:T(8,128)(2,1)} %get-tuple-element.50.wall, ...), custom_call_target="tpu_custom_call" | custom-call | tf_op jit(solution)/shard_map/pallas_call | solution.py:466
  173.9 0.9 copy-done.1
  177.7 3.5 select_select_fusion.me_ref
  181.2 25.4 %shard_map.316 = (bf16[2,256,768]{2,1,0:T(8,128)(2,1)}, f32[2,6,512,128]{3,2,1,0:T(8,128)}) custom-call(bf16[2,256,768]{2,1,0:T(8,128)(2,1)} %copy-done.1, bf16[2,2304,768]{2,1,0:T(8,128)(2,1)} %get-tuple-element.52.k_ref, bf16[2,2304,768]{2,1,0:T(8,128)(2,1)} %get-tuple-element.53.v_ref, bf16[2,2,1664,128]{3,2,1,0:T(8,128)(2,1)} %select_select_fusion.me_ref), custom_call_target="tpu_custom_call" | custom-call | tf_op jit(solution)/shard_map/pallas_call | solution.py:731
  206.6 33.4 %shard_map.317 = (bf16[512,768]{1,0:T(8,128)(2,1)}, bf16[512,768]{1,0:T(8,128)(2,1)}, f32[512,768]{1,0:T(8,128)}, bf16[768,768]{1,0:T(8,128)(2,1)}, bf16[768,307...) custom-call(bf16[512,768]{1,0:T(8,128)(2,1)} %bitcast.65, bf16[512,768]{1,0:T(8,128)(2,1)} %bitcast.61, ...), custom_call_target="tpu_custom_call" | custom-call | tf_op jit(solution)/shard_map/pallas_call | solution.py:593
  240.0 38.3 %shard_map.318 = (bf16[2,256,768]{2,1,0:T(8,128)(2,1)}, bf16[2,2304,768]{2,1,0:T(8,128)(2,1)}, bf16[2,2304,768]{2,1,0:T(8,128)(2,1)}) custom-call(bf16[2,256,768]{2,1,0:T(8,128)(2,1)} %copy-done.1, bf16[2,2304,768]{2,1,0:T(8,128)(2,1)} %get-tuple-element.52.k_ref, bf16[2,2304,768]{2,1,0:T(8,128)(2,1)} %get-tuple-element.53.v_ref, ...), custom_call_target="tpu_custom_call" | custom-call | tf_op jit(solution)/shard_map/pallas_call | solution.py:773
  278.3 39.9 %shard_map.319 = (bf16[2,2048,768]{2,1,0:T(8,128)(2,1)}, f32[2,256,768]{2,1,0:T(8,128)}, bf16[768,768]{1,0:T(8,128)(2,1)}, bf16[768,768]{1,0:T(8,128)(2,1)}, bf1...) custom-call(s32[2,19]{1,0:T(2,128)} %copy-done.3, bf16[2,2304,768]{2,1,0:T(8,128)(2,1)} %get-tuple-element.56.xs_ref, ...), custom_call_target="tpu_custom_call" | custom-call | tf_op jit(solution)/shard_map/pallas_call | solution.py:677
  318.2 0.8 convert_element_type.47
  319.0 0.8 broadcast_in_dim.170.gb
  319.8 161.5 %shard_map.320 = (f32[24,768]{1,0:T(8,128)}, f32[24,768]{1,0:T(8,128)}, f32[24,768]{1,0:T(8,128)}, f32[24,768]{1,0:T(8,128)}, f32[24,3072]{1,0:T(8,128)}, /*inde...) custom-call(bf16[8,2,48,768]{3,2,1,0:T(8,128)(2,1)} %bitcast.69, bf16[8,2,48,768]{3,2,1,0:T(8,128)(2,1)} %bitcast.70, ...), custom_call_target="tpu_custom_call" | custom-call | tf_op jit(solution)/shard_map/pallas_call | solution.py:398
  481.3 0.8 slice.46
  482.7 0.7 slice.50
  484.1 2.7 copy.95
  (88 shorter events, 10.7 us)
Async XLA Ops:
  3.9 146.4 %copy-start.3 = (s32[2,19]{1,0:T(2,128)}, s32[2,19]{1,0:T(2,128)S(1)}, u32[]{:S(2)}) copy-start(s32[2,19]{1,0:T(2,128)S(1)} %pad_add_fusion.idx) | copy-start | bytes 460
  9.7 1.2 copy-start
  150.4 23.5 %copy-start.2 = (f32[16,768]{1,0:T(8,128)}, f32[16,768]{1,0:T(8,128)S(1)}, u32[]{:S(2)}) copy-start(f32[16,768]{1,0:T(8,128)S(1)} %convert_reduce_fusion.bias) | copy-start | bytes 147460
  173.9 0.9 copy-start.1
  481.3 5.5 %copy-start.9 = (f32[24,768]{1,0:T(8,128)S(1)}, f32[24,768]{1,0:T(8,128)}, u32[]{:S(2)}) copy-start(f32[24,768]{1,0:T(8,128)} %get-tuple-element.206) | copy-start | bytes 221188
  482.1 5.3 %copy-start.8 = (f32[24,768]{1,0:T(8,128)S(1)}, f32[24,768]{1,0:T(8,128)}, u32[]{:S(2)}) copy-start(f32[24,768]{1,0:T(8,128)} %get-tuple-element.207) | copy-start | bytes 221188
  484.1 4.0 copy-start.7
  484.1 4.6 copy-start.6
  484.1 5.3 %copy-start.5 = (f32[24,3072]{1,0:T(8,128)S(1)}, f32[24,3072]{1,0:T(8,128)}, u32[]{:S(2)}) copy-start(f32[24,3072]{1,0:T(8,128)} %get-tuple-element.210) | copy-start | bytes 884740
  484.1 6.0 %copy-start.4 = (f32[96,768]{1,0:T(8,128)S(1)}, f32[96,768]{1,0:T(8,128)}, u32[]{:S(2)}) copy-start(f32[96,768]{1,0:T(8,128)} %get-tuple-element.211) | copy-start | bytes 884740
